TPU v7x, 128 devices: a whole 4x4x4 slice. The times are simulated.
128 devices in a mesh: row: 4 (over y), col: 32 (over x, z, core).
Axes of the slice: x: 4, y: 4, z: 4, core: 2. Of those that a mesh axis runs over, the one named last changes fastest.
Arguments:
- specimen: float32 [2, 2048, 16384], P(None, 'row', 'col'), may hold values from -1 to 2, as said below
- probe_field: float32 [2, 256, 256], replicated, may hold values from -6 to 6
- measured: float32 [4, 32, 8, 256, 256], P('row', 'col'), may hold values from 0 to 4
- offsets: int32 [4, 32, 8, 2], P('row', 'col'), may hold values from 0 to 511
- live_counts: int32 [4, 32], P('row', 'col'), may hold values from 1 to 8, as said below
Outputs:
- specimen_grad: float32 [2, 2048, 16384], P(None, 'row', 'col')
- probe_step: float32 [2, 256, 256], replicated
Inputs may be any that keep to these rules, and one draw needn't show every extreme that they name: `specimen`: real parts lie in 0.5 to 2 and imaginary parts in -1 to 1. `live_counts`: some device has all 8 slots live.
All inputs are finite; a program needn't handle non-finite values.
Results may differ from a plain program's by a relative error of at most 0.0003.
Values sent between devices are 32-bit elements; how exact they have to be, the bound alone decides.
A program may use at most 128 MiB of HBM per device.

v0:
```python
import math

import jax
import jax.numpy as jnp
from jax import lax
from jax.sharding import PartitionSpec as P

near_field = 0.25


def passed_along(value, axis, by):
    devices = lax.axis_size(axis)
    return lax.ppermute(value, axis, [(i, (i + by) % devices) for i in range(devices)])


def dft_tables(length):
    index_range = jnp.arange(length, dtype=jnp.int32)
    product = index_range[:, None] * index_range[None, :] % length
    angle = 2.0 * math.pi / length * product.astype(jnp.float32)
    return (jnp.cos(angle), jnp.sin(angle))


def chirp_phase(length):
    index_range = jnp.arange(length)
    wave_number = jnp.where(index_range < length // 2, index_range, index_range - length).astype(
        jnp.float32
    )
    squared = wave_number[:, None] ** 2 + wave_number[None, :] ** 2
    return -math.pi * near_field * squared / length


def left_product(table, batch):
    return jnp.einsum("ab,sbc->sac", table, batch, precision=lax.Precision.HIGHEST)


def right_product(batch, table):
    return jnp.einsum("sab,bc->sac", batch, table, precision=lax.Precision.HIGHEST)


def transform(real_part, imag_part, cosine, sine, forward):
    length = cosine.shape[0]
    table_imag = -sine if forward else sine
    mid_real = left_product(cosine, real_part) - left_product(table_imag, imag_part)
    mid_imag = left_product(cosine, imag_part) + left_product(table_imag, real_part)
    out_real = right_product(mid_real, cosine) - right_product(mid_imag, table_imag)
    out_imag = right_product(mid_imag, cosine) + right_product(mid_real, table_imag)
    if not forward:
        scale = 1.0 / (length * length)
        out_real = out_real * scale
        out_imag = out_imag * scale
    return (out_real, out_imag)


def propagate(real_part, imag_part, cosine, sine, chirp_cos, chirp_sin):
    spec_real, spec_imag = transform(real_part, imag_part, cosine, sine, True)
    turned_real = spec_real * chirp_cos - spec_imag * chirp_sin
    turned_imag = spec_real * chirp_sin + spec_imag * chirp_cos
    return transform(turned_real, turned_imag, cosine, sine, False)


def local(specimen, probe_field, measured, offsets, live_counts):
    tile_size = specimen.shape[1]
    width = probe_field.shape[1]
    slot_count = measured.shape[2]
    right = passed_along(specimen[:, :, :width], "col", -1)
    wide = jnp.concatenate([specimen, right], axis=2)
    below = passed_along(wide[:, :width, :], "row", -1)
    extended = jnp.concatenate([wide, below], axis=1)
    slot_offsets = offsets[0, 0]
    zero_index = jnp.int32(0)

    def cut_window(patch_corner):
        return lax.dynamic_slice(
            extended, (zero_index, patch_corner[0], patch_corner[1]), (2, width, width)
        )

    windows = jax.vmap(cut_window)(slot_offsets)
    obj_real = windows[:, 0]
    obj_imag = windows[:, 1]
    probe_real = probe_field[0]
    probe_imag = probe_field[1]
    active_mask = (jnp.arange(slot_count) < live_counts[0, 0]).astype(jnp.float32)[:, None, None]
    cosine, sine = dft_tables(width)
    phase = chirp_phase(width)
    chirp_cos = jnp.cos(phase)
    chirp_sin = jnp.sin(phase)
    psi_real = probe_real * obj_real - probe_imag * obj_imag
    psi_imag = probe_real * obj_imag + probe_imag * obj_real
    wave_real, wave_imag = propagate(psi_real, psi_imag, cosine, sine, chirp_cos, chirp_sin)
    model_intensity = wave_real * wave_real + wave_imag * wave_imag
    amplitude_residual = active_mask * (model_intensity - measured[0, 0])
    back_real, back_imag = propagate(
        amplitude_residual * wave_real,
        amplitude_residual * wave_imag,
        cosine,
        sine,
        chirp_cos,
        -chirp_sin,
    )
    patch_real = probe_real * back_real + probe_imag * back_imag
    patch_imag = probe_real * back_imag - probe_imag * back_real
    patches = jnp.stack([patch_real, patch_imag], axis=1)
    probe_real_sum = jnp.sum(obj_real * back_real + obj_imag * back_imag, axis=0)
    probe_imag_sum = jnp.sum(obj_real * back_imag - obj_imag * back_real, axis=0)
    probe_grad = jnp.stack([probe_real_sum, probe_imag_sum])
    illum = jnp.sum(active_mask * (obj_real * obj_real + obj_imag * obj_imag), axis=0)[None]

    def add_patch(slot_index, total):
        patch_corner = slot_offsets[slot_index]
        current = lax.dynamic_slice(
            total, (zero_index, patch_corner[0], patch_corner[1]), (2, width, width)
        )
        return lax.dynamic_update_slice(
            total, current + patches[slot_index], (zero_index, patch_corner[0], patch_corner[1])
        )

    buffer = jnp.zeros(extended.shape, jnp.float32)
    gathered = lax.fori_loop(0, slot_count, add_patch, buffer)
    spill_below = passed_along(gathered[:, tile_size:, :], "row", 1)
    wide_grad = gathered[:, :tile_size, :].at[:, :width, :].add(spill_below)
    spill_right = passed_along(wide_grad[:, :, tile_size:], "col", 1)
    specimen_grad = wide_grad[:, :, :tile_size].at[:, :, :width].add(spill_right)
    probe_total, illum_total = lax.psum((probe_grad, illum), ("row", "col"))
    probe_step = probe_total / jnp.sqrt(illum_total)
    return (specimen_grad, probe_step)


def solution(mesh):
    in_specs = (
        P(None, "row", "col"),
        P(),
        P("row", "col", None, None, None),
        P("row", "col", None, None),
        P("row", "col"),
    )
    out_specs = (P(None, "row", "col"), P())
    return jax.shard_map(local, mesh=mesh, in_specs=in_specs, out_specs=out_specs, check_vma=False)
```

profile of v0, /device:TPU:1, one launch (start us, length us, event | category | flops | bytes accessed | tf_op | source)
XLA Modules:
  0.0 557.9 jit_solution(2660203351126147284)
XLA Ops:
  10.3 13.9 %collective-permute-done = f32[2,512,256]{2,1,0:T(8,128)S(1)} collective-permute-done((f32[2,512,256]{2,1,0:T(8,128)S(1)}, f32[2,512,256]{2,1,0:T(8,128)S(1)}, u32[]{:S(2)}, u32[]{:S(2)}) %collective-permute-start) | collective-permute-done | bytes 1048608 | tf_op jit(solution)/shard_map/ppermute | solution.py:13
  25.6 2.7 collective-permute-start.1
  29.0 1.8 slice_bitcast_fusion.1
  30.9 1.9 broadcast_multiply_fusion.1
  32.7 1.8 fusion.161
  34.5 23.8 %collective-permute-done.1 = f32[2,256,768]{2,1,0:T(8,128)} collective-permute-done((f32[2,256,768]{2,1,0:T(8,128)}, f32[2,256,768]{2,1,0:T(8,128)}, u32[]{:S(2)}, u32[]{:S(2)}) %collective-permute-start.1) | collective-permute-done | bytes 1572896 | tf_op jit(solution)/shard_map/ppermute | solution.py:13
  58.3 3.8 pad_maximum_fusion
  62.2 32.0 %while.17 = (s32[]{:T(128)}, f32[2,768,768]{2,1,0:T(8,128)}, s32[8,3]{0,1:T(4,128)S(1)}, f32[8,2,256,256]{3,2,0,1:T(8,128)}, s32[]{:T(128)}) while((s32[]{:T(128)}, f32[2,768,768]{2,1,0:T(8,128)}, s32[8,3]{0,1:T(4,128)S(1)}, f32[8,2,256,256]{3,2,0,1:T(8,128)}, s32[]{:T(128)}) %tuple.69), condition=%wide.while_cond.2, body=%wide.while_body.2.sunk | while | flops 2 | bytes 1050217 | solution.py:73
  62.8 3.4 bitcast_dynamic-update-slice_fusion.2
  66.8 3.4 bitcast_dynamic-update-slice_fusion.2
  70.7 3.4 bitcast_dynamic-update-slice_fusion.2
  74.7 3.4 bitcast_dynamic-update-slice_fusion.2
  78.7 3.4 bitcast_dynamic-update-slice_fusion.2
  82.7 3.4 bitcast_dynamic-update-slice_fusion.2
  86.6 3.4 bitcast_dynamic-update-slice_fusion.2
  90.6 3.4 bitcast_dynamic-update-slice_fusion.2
  94.2 6.7 %fusion.108 = f32[8,256,256]{2,1,0:T(8,128)S(1)} fusion(f32[8,2,256,256]{3,2,0,1:T(8,128)} %get-tuple-element.113, f32[256,256]{1,0:T(8,128)S(1)} %copy-done.4, f32[256,256]{1,0:T(8,128)S(1)} %copy-done.3), kind=kOutput, calls=%fused_computation.131 | convolution fusion | flops 1613103104 | bytes 6815744 | tf_op jit(solution)/shard_map/ab,sbc->sac/dot_general | solution.py:33
  101.0 4.4 fusion.105
  105.4 4.7 convolution_add_fusion.3
  110.1 4.5 fusion.27
  114.6 4.5 fusion.25
  119.1 4.9 convolution_subtract_fusion.3
  124.0 4.5 fusion.44
  128.6 4.6 fusion.47
  133.2 4.6 fusion.67
  137.8 4.5 fusion.68
  142.2 4.8 convolution_add_fusion.2
  147.1 4.5 fusion.17
  151.6 4.5 fusion.19
  156.1 4.9 convolution_subtract_fusion.2
  160.9 4.3 add_multiply_fusion
  165.3 4.9 fusion.43
  170.2 4.5 fusion.98
  174.7 4.5 fusion.95
  179.2 4.6 convolution_add_fusion.1
  183.8 4.5 fusion.10
  188.4 4.5 fusion.8
  192.9 4.9 convolution_subtract_fusion.1
  197.8 4.6 fusion.54
  202.4 4.6 fusion.57
  207.1 4.6 fusion.69
  211.7 4.5 fusion.70
  216.2 4.8 convolution_add_fusion
  221.0 4.5 fusion.2
  225.5 4.5 fusion
  230.0 4.9 convolution_subtract_fusion
  234.9 4.3 fusion.60
  239.2 6.3 %fusion.36 = (f32[256,256]{1,0:T(8,128)S(1)}, f32[256,256]{1,0:T(8,128)}, f32[256,256]{1,0:T(8,128)}, f32[8,1,256,256]{3,2,0,1:T(8,128)S(1)}, f32[8,1,256,256]{3,2,0,1:T(8,128)S(1)}) fusion(f32[8,256,256]{2,1,0:T(8,128)S(1)} %fusion.60, f32[8,2,256,256]{3,2,0,1:T(8,128)S(1)} %copy-done, f32[8]{0:T(128)S(1)} %compare_convert_fusion, ...), kind=kOutput, calls=%fused_computation.48 | convolution fusion | flops 1622867968 | bytes 15990816 | tf_op jit(solution)/shard_map/sab,bc->sac/dot_general | solution.py:37
  245.5 2.5 pad_maximum_fusion.1
  248.1 2.4 broadcast_in_dim.4
  250.5 101.1 %while.16 = (s32[]{:T(128)}, f32[2,768,768]{2,1,0:T(8,128)}, s32[8,2]{0,1:T(2,128)S(1)}, f32[8,2,256,256]{3,2,0,1:T(8,128)}, s32[]{:T(128)}, /*index=5*/s32[]{:T(128)}, s32[]{:T(128)}) while((s32[]{:T(128)}, f32[2,768,768]{2,1,0:T(8,128)}, s32[8,2]{0,1:T(2,128)S(1)}, f32[8,2,256,256]{3,2,0,1:T(8,128)}, s32[]{:T(128)}, /*index=5*/s32[]{:T(128)}, ...), condition=%wide.region_1.2_spmd, body=%wide.region_0.1_spmd.sunk | while | flops 131080 | bytes 2621637 | solution.py:118
  256.5 6.8 %dynamic_update_slice.8 = f32[2,768,768]{2,1,0:T(8,128)} dynamic-update-slice(f32[2,768,768]{2,1,0:T(8,128)} %get-tuple-element.239, f32[2,256,256]{2,1,0:T(8,128)S(1)} %bitcast_add_fusion.2, s32[]{:T(128)} %constant.106.clone.1..sunk, s32[]{:T(128)S(6)} %select_n.247, s32[]{:T(128)S(6)} %select_n.248) | dynamic-update-slice | bytes 1048580 | tf_op jit(solution)/shard_map/while/body/eval_jaxpr/dynamic_update_slice | solution.py:113
  269.2 6.8 %dynamic_update_slice.8 = f32[2,768,768]{2,1,0:T(8,128)} dynamic-update-slice(f32[2,768,768]{2,1,0:T(8,128)} %get-tuple-element.239, f32[2,256,256]{2,1,0:T(8,128)S(1)} %bitcast_add_fusion.2, s32[]{:T(128)} %constant.106.clone.1..sunk, s32[]{:T(128)S(6)} %select_n.247, s32[]{:T(128)S(6)} %select_n.248) | dynamic-update-slice | bytes 1048580 | tf_op jit(solution)/shard_map/while/body/eval_jaxpr/dynamic_update_slice | solution.py:113
  282.0 6.3 %dynamic_update_slice.8 = f32[2,768,768]{2,1,0:T(8,128)} dynamic-update-slice(f32[2,768,768]{2,1,0:T(8,128)} %get-tuple-element.239, f32[2,256,256]{2,1,0:T(8,128)S(1)} %bitcast_add_fusion.2, s32[]{:T(128)} %constant.106.clone.1..sunk, s32[]{:T(128)S(6)} %select_n.247, s32[]{:T(128)S(6)} %select_n.248) | dynamic-update-slice | bytes 1048580 | tf_op jit(solution)/shard_map/while/body/eval_jaxpr/dynamic_update_slice | solution.py:113
  294.3 6.7 %dynamic_update_slice.8 = f32[2,768,768]{2,1,0:T(8,128)} dynamic-update-slice(f32[2,768,768]{2,1,0:T(8,128)} %get-tuple-element.239, f32[2,256,256]{2,1,0:T(8,128)S(1)} %bitcast_add_fusion.2, s32[]{:T(128)} %constant.106.clone.1..sunk, s32[]{:T(128)S(6)} %select_n.247, s32[]{:T(128)S(6)} %select_n.248) | dynamic-update-slice | bytes 1048580 | tf_op jit(solution)/shard_map/while/body/eval_jaxpr/dynamic_update_slice | solution.py:113
  307.0 6.6 %dynamic_update_slice.8 = f32[2,768,768]{2,1,0:T(8,128)} dynamic-update-slice(f32[2,768,768]{2,1,0:T(8,128)} %get-tuple-element.239, f32[2,256,256]{2,1,0:T(8,128)S(1)} %bitcast_add_fusion.2, s32[]{:T(128)} %constant.106.clone.1..sunk, s32[]{:T(128)S(6)} %select_n.247, s32[]{:T(128)S(6)} %select_n.248) | dynamic-update-slice | bytes 1048580 | tf_op jit(solution)/shard_map/while/body/eval_jaxpr/dynamic_update_slice | solution.py:113
  319.7 6.8 %dynamic_update_slice.8 = f32[2,768,768]{2,1,0:T(8,128)} dynamic-update-slice(f32[2,768,768]{2,1,0:T(8,128)} %get-tuple-element.239, f32[2,256,256]{2,1,0:T(8,128)S(1)} %bitcast_add_fusion.2, s32[]{:T(128)} %constant.106.clone.1..sunk, s32[]{:T(128)S(6)} %select_n.247, s32[]{:T(128)S(6)} %select_n.248) | dynamic-update-slice | bytes 1048580 | tf_op jit(solution)/shard_map/while/body/eval_jaxpr/dynamic_update_slice | solution.py:113
  332.4 6.4 %dynamic_update_slice.8 = f32[2,768,768]{2,1,0:T(8,128)} dynamic-update-slice(f32[2,768,768]{2,1,0:T(8,128)} %get-tuple-element.239, f32[2,256,256]{2,1,0:T(8,128)S(1)} %bitcast_add_fusion.2, s32[]{:T(128)} %constant.106.clone.1..sunk, s32[]{:T(128)S(6)} %select_n.247, s32[]{:T(128)S(6)} %select_n.248) | dynamic-update-slice | bytes 1048580 | tf_op jit(solution)/shard_map/while/body/eval_jaxpr/dynamic_update_slice | solution.py:113
  344.8 6.8 %dynamic_update_slice.8 = f32[2,768,768]{2,1,0:T(8,128)} dynamic-update-slice(f32[2,768,768]{2,1,0:T(8,128)} %get-tuple-element.239, f32[2,256,256]{2,1,0:T(8,128)S(1)} %bitcast_add_fusion.2, s32[]{:T(128)} %constant.106.clone.1..sunk, s32[]{:T(128)S(6)} %select_n.247, s32[]{:T(128)S(6)} %select_n.248) | dynamic-update-slice | bytes 1048580 | tf_op jit(solution)/shard_map/while/body/eval_jaxpr/dynamic_update_slice | solution.py:113
  353.4 2.1 slice.112
  355.4 31.6 %collective-permute-done.2 = f32[2,256,768]{2,1,0:T(8,128)S(1)} collective-permute-done((f32[2,256,768]{2,1,0:T(8,128)S(1)}, f32[2,256,768]{2,1,0:T(8,128)S(1)}, u32[]{:S(2)}, u32[]{:S(2)}) %collective-permute-start.2) | collective-permute-done | bytes 1572896 | tf_op jit(solution)/shard_map/ppermute | solution.py:13
  389.8 8.6 %collective-permute-start.3 = (f32[2,512,256]{2,1,0:T(8,128)}, f32[2,512,256]{2,1,0:T(8,128)}, u32[]{:S(2)}, u32[]{:S(2)}) collective-permute-start(f32[2,512,256]{2,1,0:T(8,128)} %slice.136), channel_id=1, source_target_pairs={{0,1},{1,2},{2,3},{3,4},{4,5},{5,6},{6,7},{7,8},{8,9},{9,10},{10,1... | collective-permute-start | bytes 3145736 | tf_op jit(solution)/shard_map/ppermute | solution.py:13
  399.2 145.8 %all-reduce.3.cloned.1.call-done = (f32[2,256,256]{2,1,0:T(8,128)}, f32[1,256,256]{2,1,0:T(8,128)}) async-done(((f32[2,256,256]{2,1,0:T(8,128)}, f32[1,256,256]{2,1,0:T(8,128)}), (f32[2,256,256]{2,1,0:T(8,128)}, f32[1,256,256]{2,1,0:T(8,128)})) %all-reduce.3.cloned.1.call-update) | async-done | bytes 786448 | tf_op jit(solution)/shard_map/psum | solution.py:123
  546.0 1.9 broadcast_divide_fusion
  (86 shorter events, 35.9 us)
Async XLA Ops:
  7.2 537.8 %all-reduce.3.cloned.1.call-start = ((), (), s32[]{:S(2)}) async-start(), calls=%async_computation | async-start | bytes 1572864 | tf_op jit(solution)/shard_map/psum | solution.py:123
  7.2 2.9 copy-start.5
  8.7 15.6 %collective-permute-start = (f32[2,512,256]{2,1,0:T(8,128)S(1)}, f32[2,512,256]{2,1,0:T(8,128)S(1)}, u32[]{:S(2)}, u32[]{:S(2)}) collective-permute-start(f32[2,512,256]{2,1,0:T(8,128)S(1)} %slice.105), channel_id=1, source_target_pairs={{0,31},{1,0},{2,1},{3,2},{4,3},{5,4},{6,5},{7,6},{8,7},{9,8},{10,9... | collective-permute-start | bytes 3145736 | tf_op jit(solution)/shard_map/ppermute | solution.py:13
  24.3 4.7 copy-start.11
  25.6 32.8 %collective-permute-start.1 = (f32[2,256,768]{2,1,0:T(8,128)}, f32[2,256,768]{2,1,0:T(8,128)}, u32[]{:S(2)}, u32[]{:S(2)}) collective-permute-start(f32[2,256,768]{2,1,0:T(8,128)} %slice.133), channel_id=1, source_target_pairs={{0,96},{32,0},{64,32},{96,64},{1,97},{33,1},{65,33},{97,65},{2,98}... | collective-permute-start | bytes 4718600 | tf_op jit(solution)/shard_map/ppermute | solution.py:13
  62.2 32.0 %copy-start.3 = (f32[256,256]{1,0:T(8,128)S(1)}, f32[256,256]{1,0:T(8,128)}, u32[]{:S(2)}) copy-start(f32[256,256]{1,0:T(8,128)} %get-tuple-element.151) | copy-start | bytes 786436
  62.2 32.0 %copy-start.4 = (f32[256,256]{1,0:T(8,128)S(1)}, f32[256,256]{1,0:T(8,128)}, u32[]{:S(2)}) copy-start(f32[256,256]{1,0:T(8,128)} %get-tuple-element.152) | copy-start | bytes 786436
  94.2 6.8 %copy-start = (f32[8,2,256,256]{3,2,0,1:T(8,128)S(1)}, f32[8,2,256,256]{3,2,0,1:T(8,128)}, u32[]{:S(2)}) copy-start(f32[8,2,256,256]{3,2,0,1:T(8,128)} %get-tuple-element.113) | copy-start | bytes 12582916
  128.5 4.6 copy-start.2
  160.9 4.3 copy-start.6
  202.4 4.6 copy-start.1
  234.9 4.3 copy-start.8
  234.9 4.3 copy-start.9
  353.1 33.9 %collective-permute-start.2 = (f32[2,256,768]{2,1,0:T(8,128)S(1)}, f32[2,256,768]{2,1,0:T(8,128)S(1)}, u32[]{:S(2)}, u32[]{:S(2)}) collective-permute-start(f32[2,256,768]{2,1,0:T(8,128)S(1)} %slice.114), channel_id=1, source_target_pairs={{0,32},{32,64},{64,96},{96,0},{1,33},{33,65},{65,97},{97,1},{2,34}... | collective-permute-start | bytes 4718600 | tf_op jit(solution)/shard_map/ppermute | solution.py:13
  388.7 9.6 %copy-start.10 = (f32[256,256]{1,0:T(8,128)S(1)}, f32[256,256]{1,0:T(8,128)}, u32[]{:S(2)}) copy-start(f32[256,256]{1,0:T(8,128)} %get-tuple-element.119) | copy-start | bytes 786436
  389.8 158.4 %collective-permute-start.3 = (f32[2,512,256]{2,1,0:T(8,128)}, f32[2,512,256]{2,1,0:T(8,128)}, u32[]{:S(2)}, u32[]{:S(2)}) collective-permute-start(f32[2,512,256]{2,1,0:T(8,128)} %slice.136), channel_id=1, source_target_pairs={{0,1},{1,2},{2,3},{3,4},{4,5},{5,6},{6,7},{7,8},{8,9},{9,10},{10,1... | collective-permute-start | bytes 3145736 | tf_op jit(solution)/shard_map/ppermute | solution.py:13
  549.5 1.3 copy-start.7
Sparse Core Ops, SparseCore 0:
  399.3 145.5 all-reduce.2
where the time goes:
time: 564 us; the launch traced here: 558 us
  waiting for transfers between devices  215 us (38%)
  matrix products  151 us (27%)
  local copies, waits for them, and re-layouts  105 us (19%)
  loops' own time  30.6 us (5%)
  other arithmetic  28.1 us (5%)
  between operations  15.4 us (3%)
  starting transfers between devices  13.1 us (2%)
    psum x1, waiting for transfers between devices, local(): probe_total, illum_total = lax.psum((probe_grad, illum), ('row', 'col'))  146 us
    dot_general x16, matrix products, left_product(): jnp.einsum('ab,sbc->sac', table, batch, precision=lax.Precision.HIGHEST)  76.9 us
    dot_general x16, matrix products, right_product(): jnp.einsum('sab,bc->sac', batch, table, precision=lax.Precision.HIGHEST)  74 us
    ppermute x4, waiting for transfers between devices, passed_along(): lax.ppermute(value, axis, [(i, (i + by) % devices) for i in range(devices)])  69.3 us
    dynamic_update_slice x8, local copies, waits for them, and re-layouts, add_patch(): lax.dynamic_update_slice(total, current + patches[slot_index], (zero_inde...  53.3 us
    gather x24, local copies, waits for them, and re-layouts  31.9 us
    another operation x1, loops' own time, local(): gathered = lax.fori_loop(0, slot_count, add_patch, buffer)  30.5 us
    ppermute x4, starting transfers between devices, passed_along(): lax.ppermute(value, axis, [(i, (i + by) % devices) for i in range(devices)])  13 us
  transfers between devices with their start and end apart: 5, of which 4 were waited for; matrix products, arithmetic and copies ran while one was open for 2% of the time, Pallas kernels for 0%

commit v1 on v0

v1 whole, which is shorter than its diff:
```python
import functools, math
import jax, jax.numpy as jnp, numpy as np, ml_dtypes
from jax import lax
from jax.experimental import pallas as pl
from jax.experimental.pallas import tpu as pltpu

W=256; T=512; S=8
BF=jnp.bfloat16
def tables():
    k=np.arange(W); k=np.where(k<W//2,k,k-W).astype(np.float64)
    h=np.exp(-1j*math.pi*0.25*k*k/W)
    a=np.fft.ifft(h)
    H=W//2
    d=(np.arange(H)[:,None]-np.arange(H)[None,:])
    out=[]
    for sgn in (1,-1):
        c=0.5*(a[d%W]+sgn*a[(d+H)%W])
        ml=np.block([[c.real,-c.imag],[c.imag,c.real]])
        out.append(ml)
    ml=np.stack(out)
    mr=np.swapaxes(ml,1,2)
    def split(m):
        hi=m.astype(np.float32).astype(ml_dtypes.bfloat16)
        lo=(m-hi.astype(np.float64)).astype(np.float32).astype(ml_dtypes.bfloat16)
        return hi,lo
    lh,ll=split(ml); rh,rl=split(mr)
    left=np.stack([np.concatenate([h_,h_,l_],axis=-1) for h_,l_ in ((lh,ll),(rh,rl))])
    right=np.stack([np.concatenate([h_,l_,h_],axis=-2) for h_,l_ in ((rh,rl),(lh,ll))])
    return left,right

def split(x):
    hi=x.astype(BF)
    lo=(x-hi.astype(jnp.float32)).astype(BF)
    return hi,lo

def right_mul(xr,xi,tab_ref,which):
    H=W//2
    outs=[]
    for n,(r,i) in enumerate(((xr[:,:H]+xr[:,H:],xi[:,:H]+xi[:,H:]),(xr[:,:H]-xr[:,H:],xi[:,:H]-xi[:,H:]))):
        s=jnp.concatenate([r,i],axis=1)
        hi,lo=split(s)
        lhs=jnp.concatenate([hi,hi,lo],axis=1)
        outs.append(jnp.dot(lhs,tab_ref[which,n],preferred_element_type=jnp.float32))
    u,v=outs
    yr=jnp.concatenate([u[:,:H]+v[:,:H],u[:,:H]-v[:,:H]],axis=1)
    yi=jnp.concatenate([u[:,H:]+v[:,H:],u[:,H:]-v[:,H:]],axis=1)
    return yr,yi

def left_mul(xr,xi,tab_ref,which):
    H=W//2
    outs=[]
    for n,(r,i) in enumerate(((xr[:H]+xr[H:],xi[:H]+xi[H:]),(xr[:H]-xr[H:],xi[:H]-xi[H:]))):
        s=jnp.concatenate([r,i],axis=0)
        hi,lo=split(s)
        rhs=jnp.concatenate([hi,lo,hi],axis=0)
        outs.append(jnp.dot(tab_ref[which,n],rhs,preferred_element_type=jnp.float32))
    u,v=outs
    yr=jnp.concatenate([u[:H]+v[:H],u[:H]-v[:H]],axis=0)
    yi=jnp.concatenate([u[H:]+v[H:],u[H:]-v[H:]],axis=0)
    return yr,yi

def kernel(offs,live,tile,right,below,corner,probe,meas,lt,rt, G,Rs,Bs,Cs,pg, ext,grad,mv,sem):
    H=W//2
    cps=[]
    for cb in range(6):
        for (top) in (True,False):
            if cb<4: src=(tile if top else below).at[:,:,pl.ds(128*cb,128)]
            else: src=(right if top else corner).at[:,:,pl.ds(128*(cb-4),128)]
            dst=ext.at[:,cb,pl.ds(0,512),:] if top else ext.at[:,cb,pl.ds(512,256),:]
            cps.append(pltpu.make_async_copy(src,dst,sem.at[len(cps)]))
    cps.append(pltpu.make_async_copy(meas,mv,sem.at[len(cps)]))
    for c in cps: c.start()
    grad[...]=jnp.zeros_like(grad)
    pg[...]=jnp.zeros_like(pg)
    for c in cps: c.wait()
    lane=lax.broadcasted_iota(jnp.int32,(W,128),1)
    def slot(s,_):
        r0=offs[2*s]; c0=offs[2*s+1]
        q=c0//128; sh=c0-q*128
        keep=lane<128-sh
        o=[]
        for ch in range(2):
            x=[pltpu.roll(ext[ch,q+j,pl.ds(r0,W),:],128-sh,1) for j in range(3)]
            o.append(jnp.concatenate([jnp.where(keep,x[0],x[1]),jnp.where(keep,x[1],x[2])],axis=1))
        orr,oi=o
        pr=probe[0]; pi=probe[1]
        ar=pr*orr-pi*oi; ai=pr*oi+pi*orr
        ar,ai=right_mul(ar,ai,rt,0)
        ar,ai=left_mul(ar,ai,lt,0)
        res=ar*ar+ai*ai-mv[s]
        ar,ai=right_mul(res*ar,res*ai,rt,1)
        br,bi=left_mul(ar,ai,lt,1)
        pg[0]+=orr*br+oi*bi
        pg[1]+=orr*bi-oi*br
        pg[2]+=orr*orr+oi*oi
        gr=pr*br+pi*bi; gi=pr*bi-pi*br
        low=lane<sh
        for ch,g in enumerate((gr,gi)):
            a=pltpu.roll(g[:,:128],sh,1); b=pltpu.roll(g[:,128:],sh,1)
            z=jnp.zeros_like(a)
            grad[ch,q,pl.ds(r0,W),:]+=jnp.where(low,z,a)
            grad[ch,q+1,pl.ds(r0,W),:]+=jnp.where(low,a,b)
            grad[ch,q+2,pl.ds(r0,W),:]+=jnp.where(low,b,z)
        return 0
    lax.fori_loop(0,live[0],slot,0)
    cps=[]
    for cb in range(6):
        for (top) in (True,False):
            if cb<4: src=(G if top else Bs).at[:,:,pl.ds(128*cb,128)]
            else: src=(Rs if top else Cs).at[:,:,pl.ds(128*(cb-4),128)]
            dst=grad.at[:,cb,pl.ds(0,512),:] if top else grad.at[:,cb,pl.ds(512,256),:]
            cps.append(pltpu.make_async_copy(dst,src,sem.at[len(cps)]))
    for c in cps: c.start()
    for c in cps: c.wait()

def compute(offs,live,tile,right,below,corner,probe,meas):
    f=jnp.float32
    left,rightt=tables()
    sd=jax.ShapeDtypeStruct
    A=pl.BlockSpec(memory_space=pl.ANY); V=pl.BlockSpec(memory_space=pltpu.VMEM); M=pl.BlockSpec(memory_space=pltpu.SMEM)
    return pl.pallas_call(kernel,
        out_shape=[sd((2,T,T),f),sd((2,T,W),f),sd((2,W,T),f),sd((2,W,W),f),sd((3,W,W),f)],
        in_specs=[M,M,A,A,A,A,V,A,V,V],out_specs=[A,A,A,A,V],
        scratch_shapes=[pltpu.VMEM((2,6,768,128),f),pltpu.VMEM((2,6,768,128),f),pltpu.VMEM((S,W,W),f),pltpu.SemaphoreType.DMA((13,))],
        compiler_params=pltpu.CompilerParams(vmem_limit_bytes=58*2**20),
    )(offs.reshape(-1),live.reshape(-1),tile,right,below,corner,probe,meas,jnp.asarray(left),jnp.asarray(rightt))


def passed_along(value, axis, by):
    devices = lax.axis_size(axis)
    return lax.ppermute(value, axis, [(i, (i + by) % devices) for i in range(devices)])


def local(specimen, probe_field, measured, offsets, live_counts):
    right = passed_along(specimen[:, :, :W], "col", -1)
    below = passed_along(specimen[:, :W, :], "row", -1)
    corner = passed_along(below[:, :, :W], "col", -1)
    G, Rs, Bs, Cs, pg = compute(offsets, live_counts, specimen, right, below, corner, probe_field, measured[0, 0])
    total = lax.psum(pg, ("row", "col"))
    spill_corner = passed_along(Cs, "col", 1)
    spill_right = passed_along(Rs, "col", 1)
    spill_below = passed_along(Bs.at[:, :, :W].add(spill_corner), "row", 1)
    grad = G.at[:, :, :W].add(spill_right).at[:, :W, :].add(spill_below)
    step = total[:2] / jnp.sqrt(total[2:])
    return (grad, step)


def solution(mesh):
    from jax.sharding import PartitionSpec as P
    in_specs = (P(None, "row", "col"), P(), P("row", "col", None, None, None), P("row", "col", None, None), P("row", "col"))
    out_specs = (P(None, "row", "col"), P())
    return jax.shard_map(local, mesh=mesh, in_specs=in_specs, out_specs=out_specs, check_vma=False)
```

time: 564 us -> 235 us (0.42)
  matrix products: 151 us -> 0 us
  local copies, waits for them, and re-layouts: 105 us -> 6.39 us
  waiting for transfers between devices: 215 us -> 179 us
  loops' own time: 30.6 us -> 0 us
  other arithmetic: 28.1 us -> 5.75 us
  Pallas kernels: 0 us -> 14.3 us
    dot_general x32 -> x0, matrix products: 151 us -> none  [the longest x16 76.9 us: left_product(): jnp.einsum('ab,sbc->sac', table, batch, precision=lax.Precision.HIGHEST)]
    dynamic_update_slice x8 -> x0, local copies, waits for them, and re-layouts: 53.3 us -> none  [add_patch(): lax.dynamic_update_slice(total, current + patches[slot_index], (zero_inde...]
    ppermute x4 -> x6, waiting for transfers between devices: 69.3 us -> 33 us  [passed_along(): lax.ppermute(value, axis, [(i, (i + by) % devices) for i in range(devices)])]
    gather x24 -> x0, local copies, waits for them, and re-layouts: 31.9 us -> none
    another operation x2 -> x0, loops' own time: 30.6 us -> none  [the longest x1 30.5 us: local(): gathered = lax.fori_loop(0, slot_count, add_patch, buffer)]
    pallas_call x0 -> x1, Pallas kernels: none -> 14.3 us  [compute(): pl.pallas_call(kernel, out_shape=[sd((2, T, T), f), sd((2, T, W), f), sd(...]
    add x8 -> x0, other arithmetic: 12.3 us -> none  [add_patch(): current + patches[slot_index]]
    slice x14 -> x3, local copies, waits for them, and re-layouts: 12.1 us -> 2.54 us  [the longest x1 1.44 us: local(): below = passed_along(specimen[:, :W, :], 'row', -1)]
  transfers between devices with their start and end apart: 5 -> 7, of which waited for: 4 -> 4; matrix products, arithmetic and copies ran while one was open for 2% -> 3% of each run, Pallas kernels for 0% -> 0%
where the time goes in v1:
time: 235 us; the launch traced here: 234 us
  waiting for transfers between devices  179 us (76%)
  between operations  14.8 us (6%)
  starting transfers between devices  14.3 us (6%)
  Pallas kernels  14.3 us (6%)
  local copies, waits for them, and re-layouts  6.39 us (3%)
  other arithmetic  5.75 us (2%)
    psum x1, waiting for transfers between devices, local(): total = lax.psum(pg, ('row', 'col'))  146 us
    ppermute x6, waiting for transfers between devices, passed_along(): lax.ppermute(value, axis, [(i, (i + by) % devices) for i in range(devices)])  33 us
    pallas_call x1, Pallas kernels, compute(): pl.pallas_call(kernel, out_shape=[sd((2, T, T), f), sd((2, T, W), f), sd(...  14.3 us
    ppermute x6, starting transfers between devices, passed_along(): lax.ppermute(value, axis, [(i, (i + by) % devices) for i in range(devices)])  14.2 us
  transfers between devices with their start and end apart: 7, of which 4 were waited for; matrix products, arithmetic and copies ran while one was open for 3% of the time, Pallas kernels for 0%

profile of v1, /device:TPU:1, one launch (start us, length us, event | category | flops | bytes accessed | tf_op | source)
XLA Modules:
  0.0 234.4 jit_solution(17580660182029253375)
XLA Ops:
  7.2 0.0 copy-start
  7.2 0.0 all-reduce.2.cloned.1.call-start
  7.2 1.4 slice.88
  8.7 0.0 copy-start.6
  8.7 3.6 %collective-permute-start.1 = (f32[2,256,512]{2,1,0:T(8,128)S(1)}, f32[2,256,512]{2,1,0:T(8,128)S(1)}, u32[]{:S(2)}, u32[]{:S(2)}) collective-permute-start(f32[2,256,512]{2,1,0:T(8,128)S(1)} %slice.88), channel_id=1, source_target_pairs={{0,96},{32,0},{64,32},{96,64},{1,97},{33,1},{65,33},{97,65},{2,98}... | collective-permute-start | bytes 3145736 | tf_op jit(solution)/shard_map/ppermute | solution.py:131
  12.3 0.0 copy-done
  12.3 1.1 slice.87
  13.4 1.0 collective-permute-start
  14.3 19.8 %collective-permute-done.1.below = f32[2,256,512]{2,1,0:T(8,128)S(1)} collective-permute-done((f32[2,256,512]{2,1,0:T(8,128)S(1)}, f32[2,256,512]{2,1,0:T(8,128)S(1)}, u32[]{:S(2)}, u32[]{:S(2)}) %collective-permute-start.1) | collective-permute-done | bytes 1048608 | tf_op jit(solution)/shard_map/ppermute | solution.py:131
  34.1 0.0 copy-start.1
  34.2 1.6 collective-permute-start.2
  36.4 0.0 copy-done.6
  36.5 0.1 copy.10
  36.5 0.6 reshape.99.offs
  37.2 0.0 collective-permute-done.right
  37.2 0.0 copy-start.4
  37.2 7.0 %collective-permute-done.2.corner = f32[2,256,256]{2,1,0:T(8,128)S(1)} collective-permute-done((f32[2,256,256]{2,1,0:T(8,128)S(1)}, f32[2,256,256]{2,1,0:T(8,128)S(1)}, u32[]{:S(2)}, u32[]{:S(2)}) %collective-permute-start.2) | collective-permute-done | bytes 524320 | tf_op jit(solution)/shard_map/ppermute | solution.py:131
  44.2 0.0 copy-start.5
  44.2 0.0 copy-done.1
  44.2 0.0 copy-done.4
  44.2 0.8 copy-done.5
  45.0 14.3 %shard_map.86 = (f32[2,512,512]{2,1,0:T(8,128)}, f32[2,512,256]{2,1,0:T(8,128)}, f32[2,256,512]{2,1,0:T(8,128)}, f32[2,256,256]{2,1,0:T(8,128)}, f32[3,256,256]{2,1,0:T(8,128)}) custom-call(s32[16]{0:T(128)} %reshape.99.offs, s32[1]{0:T(128)} %bitcast.6.live, f32[2,512,512]{2,1,0:T(8,128)} %tile.1, f32[2,512,256]{2,1,0:T(8,128)} %copy-done.4, ...), custom_call_target="tpu_custom_call" | custom-call | tf_op jit(solution)/shard_map/pallas_call | solution.py:121
  59.3 7.8 %collective-permute-start.4 = (f32[2,256,256]{2,1,0:T(8,128)}, f32[2,256,256]{2,1,0:T(8,128)}, u32[]{:S(2)}, u32[]{:S(2)}) collective-permute-start(f32[2,256,256]{2,1,0:T(8,128)} %get-tuple-element.46), channel_id=1, source_target_pairs={{0,1},{1,2},{2,3},{3,4},{4,5},{5,6},{6,7},{7,8},{8,9},{9,10},{10,1... | collective-permute-start | bytes 1572872 | tf_op jit(solution)/shard_map/ppermute | solution.py:131
  67.1 0.2 collective-permute-start.3
  67.3 0.0 copy-start.2
  67.3 0.0 all-reduce.2.cloned.1.call-update
  67.3 6.2 %collective-permute-done.4 = f32[2,256,256]{2,1,0:T(8,128)} collective-permute-done((f32[2,256,256]{2,1,0:T(8,128)}, f32[2,256,256]{2,1,0:T(8,128)}, u32[]{:S(2)}, u32[]{:S(2)}) %collective-permute-start.4) | collective-permute-done | bytes 524320 | tf_op jit(solution)/shard_map/ppermute | solution.py:131
  73.6 2.1 add_dynamic-update-slice_fusion.1
  75.7 0.0 collective-permute-start.5
  75.7 145.8 %all-reduce.2.cloned.1.call-done = f32[3,256,256]{2,1,0:T(8,128)} async-done(((f32[3,256,256]{2,1,0:T(8,128)}), f32[3,256,256]{2,1,0:T(8,128)}) %all-reduce.2.cloned.1.call-update) | async-done | bytes 786448 | tf_op jit(solution)/shard_map/psum | solution.py:139
  221.5 1.0 fusion.1
  222.5 1.9 slice_divide_fusion
  224.4 0.0 collective-permute-done.3
  224.4 0.0 copy-done.2
  224.4 0.3 add_dynamic-update-slice_fusion
  224.7 0.0 collective-permute-done.5
  224.7 1.5 fusion
  226.2 0.0 copy-start.3
  226.2 1.3 copy-done.3
  (1 shorter events, 0.0 us)
Async XLA Ops:
  7.2 5.1 %copy-start = (f32[2,512,512]{2,1,0:T(8,128)S(1)}, f32[2,512,512]{2,1,0:T(8,128)}, u32[]{:S(2)}) copy-start(f32[2,512,512]{2,1,0:T(8,128)} %tile.1) | copy-start | bytes 6291460
  7.2 214.3 %all-reduce.2.cloned.1.call-start = ((), (), s32[]{:S(2)}) async-start(), calls=%async_computation | async-start | bytes 1572864 | tf_op jit(solution)/shard_map/psum | solution.py:139
  8.7 27.8 %copy-start.6 = (s32[1,1,8,2]{2,3,1,0:T(2,128)S(1)}, s32[1,1,8,2]{2,3,1,0:T(2,128)}, u32[]{:S(2)}) copy-start(s32[1,1,8,2]{2,3,1,0:T(2,128)} %param.16) | copy-start | bytes 196
  8.7 25.5 %collective-permute-start.1 = (f32[2,256,512]{2,1,0:T(8,128)S(1)}, f32[2,256,512]{2,1,0:T(8,128)S(1)}, u32[]{:S(2)}, u32[]{:S(2)}) collective-permute-start(f32[2,256,512]{2,1,0:T(8,128)S(1)} %slice.88), channel_id=1, source_target_pairs={{0,96},{32,0},{64,32},{96,64},{1,97},{33,1},{65,33},{97,65},{2,98}... | collective-permute-start | bytes 3145736 | tf_op jit(solution)/shard_map/ppermute | solution.py:131
  13.4 23.8 %collective-permute-start = (f32[2,512,256]{2,1,0:T(8,128)}, f32[2,512,256]{2,1,0:T(8,128)S(1)}, u32[]{:S(2)}, u32[]{:S(2)}) collective-permute-start(f32[2,512,256]{2,1,0:T(8,128)} %slice.87), channel_id=1, source_target_pairs={{0,31},{1,0},{2,1},{3,2},{4,3},{5,4},{6,5},{7,6},{8,7},{9,8},{10,9... | collective-permute-start | bytes 3145736 | tf_op jit(solution)/shard_map/ppermute | solution.py:131
  34.1 10.0 %copy-start.1 = (f32[2,256,512]{2,1,0:T(8,128)}, f32[2,256,512]{2,1,0:T(8,128)S(1)}, u32[]{:S(2)}) copy-start(f32[2,256,512]{2,1,0:T(8,128)S(1)} %collective-permute-done.1.below) | copy-start | bytes 3145732
  34.2 10.0 %collective-permute-start.2 = (f32[2,256,256]{2,1,0:T(8,128)S(1)}, f32[2,256,256]{2,1,0:T(8,128)S(1)}, u32[]{:S(2)}, u32[]{:S(2)}) collective-permute-start(f32[2,256,256]{2,1,0:T(8,128)S(1)} %slice.95), channel_id=1, source_target_pairs={{0,31},{1,0},{2,1},{3,2},{4,3},{5,4},{6,5},{7,6},{8,7},{9,8},{10,9... | collective-permute-start | bytes 1572872 | tf_op jit(solution)/shard_map/ppermute | solution.py:131
  37.2 7.0 %copy-start.4 = (f32[2,512,256]{2,1,0:T(8,128)}, f32[2,512,256]{2,1,0:T(8,128)S(1)}, u32[]{:S(2)}) copy-start(f32[2,512,256]{2,1,0:T(8,128)S(1)} %collective-permute-done.right) | copy-start | bytes 3145732
  44.2 0.8 copy-start.5
  59.3 14.3 %collective-permute-start.4 = (f32[2,256,256]{2,1,0:T(8,128)}, f32[2,256,256]{2,1,0:T(8,128)}, u32[]{:S(2)}, u32[]{:S(2)}) collective-permute-start(f32[2,256,256]{2,1,0:T(8,128)} %get-tuple-element.46), channel_id=1, source_target_pairs={{0,1},{1,2},{2,3},{3,4},{4,5},{5,6},{6,7},{7,8},{8,9},{9,10},{10,1... | collective-permute-start | bytes 1572872 | tf_op jit(solution)/shard_map/ppermute | solution.py:131
  67.1 157.3 %collective-permute-start.3 = (f32[2,512,256]{2,1,0:T(8,128)}, f32[2,512,256]{2,1,0:T(8,128)S(1)}, u32[]{:S(2)}, u32[]{:S(2)}) collective-permute-start(f32[2,512,256]{2,1,0:T(8,128)} %get-tuple-element.44), channel_id=1, source_target_pairs={{0,1},{1,2},{2,3},{3,4},{4,5},{5,6},{6,7},{7,8},{8,9},{9,10},{10,1... | collective-permute-start | bytes 3145736 | tf_op jit(solution)/shard_map/ppermute | solution.py:131
  67.3 157.1 %copy-start.2 = (f32[2,512,512]{2,1,0:T(8,128)S(1)}, f32[2,512,512]{2,1,0:T(8,128)}, u32[]{:S(2)}) copy-start(f32[2,512,512]{2,1,0:T(8,128)} %get-tuple-element.43) | copy-start | bytes 6291460
  75.7 149.0 %collective-permute-start.5 = (f32[2,256,512]{2,1,0:T(8,128)}, f32[2,256,512]{2,1,0:T(8,128)}, u32[]{:S(2)}, u32[]{:S(2)}) collective-permute-start(f32[2,256,512]{2,1,0:T(8,128)} %add_dynamic-update-slice_fusion.1), channel_id=1, source_target_pairs={{0,32},{32,64},{64,96},{96,0},{1,33},{33,65},{65,97},{97,1},{2,34}... | collective-permute-start | bytes 3145736 | tf_op jit(solution)/shard_map/ppermute | solution.py:131
  226.2 1.3 copy-start.3
Sparse Core Ops, SparseCore 0:
  67.5 153.9 all-reduce.1

commit v2 on v1

--- a/solution.py
+++ b/solution.py
@@ -126,22 +126,208 @@
     )(offs.reshape(-1),live.reshape(-1),tile,right,below,corner,probe,meas,jnp.asarray(left),jnp.asarray(rightt))
 
 
-def passed_along(value, axis, by):
-    devices = lax.axis_size(axis)
-    return lax.ppermute(value, axis, [(i, (i + by) % devices) for i in range(devices)])
+MESH = pl.DeviceIdType.MESH
+
+
+def put(src, dst, send, recv, device):
+    return pltpu.make_async_remote_copy(src_ref=src, dst_ref=dst, send_sem=send, recv_sem=recv, device_id=device, device_id_type=MESH)
+
+
+def places():
+    row, col = lax.axis_index("row"), lax.axis_index("col")
+    rows, cols = lax.axis_size("row"), lax.axis_size("col")
+    return row, col, ((row + rows - 1) % rows, col), ((row + 1) % rows, col), (row, (col + cols - 1) % cols), (row, (col + 1) % cols)
+
+
+def greet(devices):
+    barrier = pltpu.get_barrier_semaphore()
+    for device in devices:
+        pl.semaphore_signal(barrier, inc=1, device_id=device, device_id_type=MESH)
+    return barrier
+
+
+def halo_kernel(tile, R, B, X, hop1, hop2, snd, rcv):
+    row, col, up, down, left, right = places()
+    pl.semaphore_wait(greet((up, down, left, right)), 4)
+    n = [0]
+
+    def send(src, dst, device):
+        k = n[0]
+        n[0] += 1
+        c = put(src, dst, snd.at[k], rcv.at[k], device)
+        c.start()
+        return c
+
+    H = W // 2
+    Q = H // 2
+    near = [pl.ds(H * k, H) for k in range(2)]
+    far = [pl.ds(H + Q * k, Q) for k in range(2)]
+    lo, hi = pl.ds(0, W), pl.ds(W, W)
+    first = [send(tile.at[:, far[k], hi], hop1.at[k], down) for k in range(2)]
+    b = [send(tile.at[:, near[k], lo], B.at[:, near[k], lo], up) for k in range(2)]
+    r = send(tile.at[:, :, lo], R, left)
+    b2 = send(tile.at[:, near[0], hi], B.at[:, near[0], hi], up)
+    second, third, x = [], [], []
+    for k in range(2):
+        first[k].wait_recv()
+        second.append(send(hop1.at[k], hop2.at[k], down))
+    for k in range(2):
+        b[k].wait_recv()
+        x.append(send(B.at[:, near[k], lo], X.at[:, near[k], :], left))
+        second[k].wait_recv()
+        third.append(send(hop2.at[k], B.at[:, far[k], hi], down))
+    for c in (r, b2, *third, *x):
+        c.wait_recv()
+    for c in (*first, *b, r, b2, *second, *third, *x):
+        c.wait_send()
+
+
+def halos(tile):
+    f = jnp.float32
+    A = pl.BlockSpec(memory_space=pl.ANY)
+    sd = jax.ShapeDtypeStruct
+    return pl.pallas_call(halo_kernel, out_shape=[sd((2, T, W), f), sd((2, W, T), f), sd((2, W, W), f)],
+        in_specs=[A], out_specs=[A, A, A],
+        scratch_shapes=[pltpu.VMEM((2, 2, W // 4, W), f), pltpu.VMEM((2, 2, W // 4, W), f), pltpu.SemaphoreType.DMA((12,)), pltpu.SemaphoreType.DMA((12,))],
+        compiler_params=pltpu.CompilerParams(collective_id=0, has_side_effects=True, vmem_limit_bytes=58*2**20))(tile)
+
+
+def spill_kernel(Rs, Bs, Cs, pg, RR, BR, step, hop1, hop2, corner, bleft, mine, half, acc, plane, part, ybuf, shard, loc, snd, rcv, psnd, prcv, gsnd, grcv):
+    row, col, up, down, left, right = places()
+    rows, chips = lax.axis_size("row"), lax.axis_size("col") // 2
+    core, chip = col % 2, col // 2
+    sib = (row, col + 1 - 2 * core)
+    H = W // 2
+    Q = H // 2
+    step_rows = H // chips
+
+    def peer(j):
+        return (row, ((chip + j) % chips) * 2 + core)
+
+    barrier = greet((up, down, left, right, sib, ((row + 2) % rows, col)))
+
+    def hello(j, _):
+        pl.semaphore_signal(barrier, inc=1, device_id=peer(j), device_id_type=MESH)
+        return 0
+
+    lax.fori_loop(1, chips, hello, 0)
+    bl = pltpu.make_async_copy(Bs.at[:, :, pl.ds(0, W)], bleft, loc.at[0])
+    bl.start()
+    ml = pltpu.make_async_copy(pg.at[:, pl.ds(core * H, H), :], mine, loc.at[1])
+    ml.start()
+    pl.semaphore_wait(barrier, 6 + chips - 1)
+    n = [0]
+
+    def send(src, dst, device):
+        k = n[0]
+        n[0] += 1
+        c = put(src, dst, snd.at[k], rcv.at[k], device)
+        c.start()
+        return c
+
+    near = [pl.ds(H * k, H) for k in range(2)]
+    far = [pl.ds(H + Q * k, Q) for k in range(2)]
+    lo, hi = pl.ds(0, W), pl.ds(W, W)
+    s1 = send(pg.at[:, pl.ds((1 - core) * H, H), :], half, sib)
+    sc = send(Cs, corner, right)
+    first = [send(Bs.at[:, far[k], hi], hop1.at[k], up) for k in range(2)]
+    b2 = send(Bs.at[:, near[0], hi], BR.at[:, near[0], hi], down)
+    ml.wait()
+    s1.wait_recv()
+    acc[...] = mine[...] + half[...]
+
+    def shard_of(j):
+        p = (chip + j) % chips
+        return put(acc.at[:, pl.ds(pl.multiple_of(p * step_rows, step_rows), step_rows), :], plane.at[j], psnd.at[j], prcv.at[j], peer(j))
+
+    def begin(j, _):
+        shard_of(j).start()
+        return 0
+
+    lax.fori_loop(1, chips, begin, 0)
+    r = send(Rs, RR, right)
+    second, third = [], []
+    for k in range(2):
+        first[k].wait_recv()
+        second.append(send(hop1.at[k], hop2.at[k], up))
+    bl.wait()
+    sc.wait_recv()
+    bleft[...] += corner[...]
+    b = send(bleft, BR.at[:, :, lo], down)
+
+    part[...] = acc[:, pl.ds(pl.multiple_of(chip * step_rows, step_rows), step_rows), :]
+
+    def collect(j, _):
+        shard_of(j).wait_recv()
+        part[...] += plane[j]
+        return 0
+
+    lax.fori_loop(1, chips, collect, 0)
+    ys = [send(part, ybuf.at[row], ((row + k) % rows, col)) for k in range(1, 4)]
+    ybuf[pl.ds(row, 1)] = part[...][None]
+    for k in range(2):
+        second[k].wait_recv()
+        third.append(send(hop2.at[k], BR.at[:, far[k], hi], up))
+    for y in ys:
+        y.wait_recv()
+    total = ybuf[0] + ybuf[1] + ybuf[2] + ybuf[3]
+    shard[...] = total[:2] / jnp.sqrt(total[2:])
+
+    here = pl.ds(pl.multiple_of(core * H + chip * step_rows, step_rows), step_rows)
+    own = pltpu.make_async_copy(shard, step.at[:, here, :], loc.at[2])
+    own.start()
+
+    def gather(j):
+        return put(shard, step.at[:, here, :], gsnd.at[j], grcv.at[j], peer(j))
+
+    def begin2(j, _):
+        gather(j).start()
+        return 0
+
+    lax.fori_loop(1, chips, begin2, 0)
+
+    def collect2(j, _):
+        gather(j).wait_recv()
+        return 0
+
+    lax.fori_loop(1, chips, collect2, 0)
+    own.wait()
+    mine_rows = pl.ds(pl.multiple_of(core * H, H), H)
+    s5 = send(step.at[:, mine_rows, :], step.at[:, mine_rows, :], sib)
+    for c in (r, b2, b, *third, s5):
+        c.wait_recv()
+
+    def drain(j, _):
+        shard_of(j).wait_send()
+        gather(j).wait_send()
+        return 0
+
+    lax.fori_loop(1, chips, drain, 0)
+    for c in (s1, sc, r, b2, b, *first, *second, *third, *ys, s5):
+        c.wait_send()
+
+
+def spills(Rs, Bs, Cs, pg, rows, cols):
+    f = jnp.float32
+    chips = cols // 2
+    A = pl.BlockSpec(memory_space=pl.ANY)
+    sd = jax.ShapeDtypeStruct
+    V = pltpu.VMEM
+    D = pltpu.SemaphoreType.DMA
+    sh = W // 2 // chips
+    return pl.pallas_call(spill_kernel, out_shape=[sd((2, T, W), f), sd((2, W, T), f), sd((2, W, W), f)],
+        in_specs=[A] * 4, out_specs=[A, A, A],
+        scratch_shapes=[V((2, 2, W // 4, W), f), V((2, 2, W // 4, W), f), V((2, W, W), f), V((2, W, W), f),
+            V((3, W // 2, W), f), V((3, W // 2, W), f), V((3, W // 2, W), f), V((chips, 3, sh, W), f), V((3, sh, W), f), V((rows, 3, sh, W), f), V((2, sh, W), f),
+            D((3,)), D((15,)), D((15,)), D((chips,)), D((chips,)), D((chips,)), D((chips,))],
+        compiler_params=pltpu.CompilerParams(collective_id=1, has_side_effects=True, vmem_limit_bytes=58*2**20))(Rs, Bs, Cs, pg)
 
 
 def local(specimen, probe_field, measured, offsets, live_counts):
-    right = passed_along(specimen[:, :, :W], "col", -1)
-    below = passed_along(specimen[:, :W, :], "row", -1)
-    corner = passed_along(below[:, :, :W], "col", -1)
+    right, below, corner = halos(specimen)
     G, Rs, Bs, Cs, pg = compute(offsets, live_counts, specimen, right, below, corner, probe_field, measured[0, 0])
-    total = lax.psum(pg, ("row", "col"))
-    spill_corner = passed_along(Cs, "col", 1)
-    spill_right = passed_along(Rs, "col", 1)
-    spill_below = passed_along(Bs.at[:, :, :W].add(spill_corner), "row", 1)
-    grad = G.at[:, :, :W].add(spill_right).at[:, :W, :].add(spill_below)
-    step = total[:2] / jnp.sqrt(total[2:])
+    from_left, from_above, step = spills(Rs, Bs, Cs, pg, lax.axis_size("row"), lax.axis_size("col"))
+    grad = G.at[:, :, :W].add(from_left).at[:, :W, :].add(from_above)
     return (grad, step)
 
 

time: 235 us -> 93.1 us (0.40)
  waiting for transfers between devices: 179 us -> 0 us
  Pallas kernels: 14.3 us -> 86.1 us
  starting transfers between devices: 14.3 us -> 0 us
  between operations: 14.8 us -> 1.35 us
  other arithmetic: 5.75 us -> 1.86 us
  local copies, waits for them, and re-layouts: 6.39 us -> 3.61 us
    psum x1 -> x0, waiting for transfers between devices: 146 us -> none  [local(): total = lax.psum(pg, ('row', 'col'))]
    pallas_call x0 -> x2, Pallas kernels: none -> 65.9 us  [the longest x1 40.9 us: spills(): pl.pallas_call(spill_kernel, out_shape=[sd((2, T, W), f), sd((2, W, T), f...]
    ppermute x6 -> x0, waiting for transfers between devices: 33 us -> none  [passed_along(): lax.ppermute(value, axis, [(i, (i + by) % devices) for i in range(devices)])]
    ppermute x6 -> x0, starting transfers between devices: 14.2 us -> none  [passed_along(): lax.ppermute(value, axis, [(i, (i + by) % devices) for i in range(devices)])]
    pallas_call x1, Pallas kernels: 14.3 us -> 20.2 us  [compute(): pl.pallas_call(kernel, out_shape=[sd((2, T, T), f), sd((2, T, W), f), sd(...]
    slice x3 -> x0, local copies, waits for them, and re-layouts: 2.54 us -> none  [the longest x1 1.44 us: local(): below = passed_along(specimen[:, :W, :], 'row', -1)]
  transfers between devices with their start and end apart: 7 -> 0, of which waited for: 4 -> 0; matrix products, arithmetic and copies ran while one was open for 3% -> 0% of each run, Pallas kernels for 0% -> 0%
where the time goes in v2:
time: 93.1 us; the launch traced here: 92.9 us
  Pallas kernels  86.1 us (92%)
  local copies, waits for them, and re-layouts  3.61 us (4%)
  other arithmetic  1.86 us (2%)
  between operations  1.35 us (1%)
    pallas_call x1, Pallas kernels, spills(): pl.pallas_call(spill_kernel, out_shape=[sd((2, T, W), f), sd((2, W, T), f...  40.9 us
    pallas_call x1, Pallas kernels, halos(): pl.pallas_call(halo_kernel, out_shape=[sd((2, T, W), f), sd((2, W, T), f)...  25 us
    pallas_call x1, Pallas kernels, compute(): pl.pallas_call(kernel, out_shape=[sd((2, T, T), f), sd((2, T, W), f), sd(...  20.2 us
    unnamed x10, local copies, waits for them, and re-layouts  3 us

profile of v2, /device:TPU:1, one launch (start us, length us, event | category | flops | bytes accessed | tf_op | source)
XLA Modules:
  0.0 92.9 jit_solution(2170961475983092788)
XLA Ops:
  1.3 0.8 copy.10
  2.0 0.6 reshape.71.offs
  2.6 25.0 %shard_map.86 = (f32[2,512,256]{2,1,0:T(8,128)}, f32[2,256,512]{2,1,0:T(8,128)}, f32[2,256,256]{2,1,0:T(8,128)}) custom-call(f32[2,512,512]{2,1,0:T(8,128)} %tile.3), custom_call_target="tpu_custom_call" | custom-call | tf_op jit(solution)/shard_map/pallas_call | solution.py:189
  27.7 20.2 %shard_map.87 = (f32[2,512,512]{2,1,0:T(8,128)}, f32[2,512,256]{2,1,0:T(8,128)}, f32[2,256,512]{2,1,0:T(8,128)}, f32[2,256,256]{2,1,0:T(8,128)}, f32[3,256,256]{2,1,0:T(8,128)}) custom-call(s32[16]{0:T(128)} %reshape.71.offs, s32[1]{0:T(128)} %bitcast.4.live, f32[2,512,512]{2,1,0:T(8,128)} %tile.3, f32[2,512,256]{2,1,0:T(8,128)} %get-tuple-element.37.right, ...), custom_call_target="tpu_custom_call" | custom-call | tf_op jit(solution)/shard_map/pallas_call | solution.py:121
  47.9 0.0 copy-start
  47.9 40.9 %shard_map.88 = (f32[2,512,256]{2,1,0:T(8,128)}, f32[2,256,512]{2,1,0:T(8,128)}, f32[2,256,256]{2,1,0:T(8,128)}) custom-call(f32[2,512,256]{2,1,0:T(8,128)} %get-tuple-element.41.Rs, f32[2,256,512]{2,1,0:T(8,128)} %get-tuple-element.42.Bs, f32[2,256,256]{2,1,0:T(8,128)} %get-tuple-element.43.Cs, f32[3,256,256]{2,1,0:T(8,128)} %get-tuple-element.44.pg), custom_call_target="tpu_custom_call" | custom-call | tf_op jit(solution)/shard_map/pallas_call | solution.py:318
  88.7 0.0 copy-start.2
  88.7 0.0 copy-done
  88.8 1.6 %add_dynamic-update-slice_fusion = f32[2,512,512]{2,1,0:T(8,128)S(1)} fusion(f32[2,512,512]{2,1,0:T(8,128)S(1)} %copy-done, f32[2,512,256]{2,1,0:T(8,128)} %get-tuple-element.45), kind=kLoop, calls=%fused_computation.2 | loop fusion | flops 262144 | bytes 3145728 | tf_op jit(solution)/shard_map/scatter-add | solution.py:330
  90.3 0.0 copy-done.2
  90.4 0.0 copy-start.3
  90.4 0.3 fusion
  90.6 0.7 copy-done.3
  91.4 0.0 copy-start.1
  91.4 0.8 copy.15
  92.2 0.7 copy-done.1
Async XLA Ops:
  47.9 40.9 %copy-start = (f32[2,512,512]{2,1,0:T(8,128)S(1)}, f32[2,512,512]{2,1,0:T(8,128)}, u32[]{:S(2)}) copy-start(f32[2,512,512]{2,1,0:T(8,128)} %get-tuple-element.40) | copy-start | bytes 6291460
  88.7 1.6 %copy-start.2 = (f32[2,256,512]{2,1,0:T(8,128)S(1)}, f32[2,256,512]{2,1,0:T(8,128)}, u32[]{:S(2)}) copy-start(f32[2,256,512]{2,1,0:T(8,128)} %get-tuple-element.46) | copy-start | bytes 3145732
  90.4 1.0 %copy-start.3 = (f32[2,256,256]{2,1,0:T(8,128)S(1)}, f32[2,256,256]{2,1,0:T(8,128)}, u32[]{:S(2)}) copy-start(f32[2,256,256]{2,1,0:T(8,128)} %get-tuple-element.51) | copy-start | bytes 1572868
  91.4 1.5 %copy-start.1 = (f32[2,512,512]{2,1,0:T(8,128)}, f32[2,512,512]{2,1,0:T(8,128)S(1)}, u32[]{:S(2)}) copy-start(f32[2,512,512]{2,1,0:T(8,128)S(1)} %fusion) | copy-start | bytes 6291460

commit v3 on v2

v3 whole, which is shorter than its diff:
```python
import functools, math
import jax, jax.numpy as jnp, numpy as np, ml_dtypes
from jax import lax
from jax.experimental import pallas as pl
from jax.experimental.pallas import tpu as pltpu

W=256; T=512; S=8
VM2=24
BF=jnp.bfloat16
def tables():
    k=np.arange(W); k=np.where(k<W//2,k,k-W).astype(np.float64)
    h=np.exp(-1j*math.pi*0.25*k*k/W)
    a=np.fft.ifft(h)
    H=W//2
    d=(np.arange(H)[:,None]-np.arange(H)[None,:])
    out=[]
    for sgn in (1,-1):
        c=0.5*(a[d%W]+sgn*a[(d+H)%W])
        ml=np.block([[c.real,-c.imag],[c.imag,c.real]])
        out.append(ml)
    ml=np.stack(out)
    mr=np.swapaxes(ml,1,2)
    def split(m):
        hi=m.astype(np.float32).astype(ml_dtypes.bfloat16)
        lo=(m-hi.astype(np.float64)).astype(np.float32).astype(ml_dtypes.bfloat16)
        return hi,lo
    lh,ll=split(ml); rh,rl=split(mr)
    return np.stack([lh,rh]),np.stack([ll,rl])

def split(x):
    hi=x.astype(BF)
    lo=(x-hi.astype(jnp.float32)).astype(BF)
    return hi,lo

def right_mul(xr,xi,th,tl,which):
    H=W//2
    outs=[]
    for n,(r,i) in enumerate(((xr[:,:H]+xr[:,H:],xi[:,:H]+xi[:,H:]),(xr[:,:H]-xr[:,H:],xi[:,:H]-xi[:,H:]))):
        s=jnp.concatenate([r,i],axis=1)
        hi,lo=split(s)
        lhs=jnp.concatenate([hi,hi,lo],axis=1)
        outs.append(jnp.dot(lhs,jnp.concatenate([th[1-which,n],tl[1-which,n],th[1-which,n]],axis=0),preferred_element_type=jnp.float32))
    u,v=outs
    yr=jnp.concatenate([u[:,:H]+v[:,:H],u[:,:H]-v[:,:H]],axis=1)
    yi=jnp.concatenate([u[:,H:]+v[:,H:],u[:,H:]-v[:,H:]],axis=1)
    return yr,yi

def left_mul(xr,xi,th,tl,which):
    H=W//2
    outs=[]
    for n,(r,i) in enumerate(((xr[:H]+xr[H:],xi[:H]+xi[H:]),(xr[:H]-xr[H:],xi[:H]-xi[H:]))):
        s=jnp.concatenate([r,i],axis=0)
        hi,lo=split(s)
        rhs=jnp.concatenate([hi,lo,hi],axis=0)
        outs.append(jnp.dot(jnp.concatenate([th[which,n],th[which,n],tl[which,n]],axis=1),rhs,preferred_element_type=jnp.float32))
    u,v=outs
    yr=jnp.concatenate([u[:H]+v[:H],u[:H]-v[:H]],axis=0)
    yi=jnp.concatenate([u[H:]+v[H:],u[H:]-v[H:]],axis=0)
    return yr,yi

def kernel(offs,live,ext,probe,mv,th,tl, grad,pg):
    grad[...]=jnp.zeros_like(grad)
    pg[...]=jnp.zeros_like(pg)
    lane=lax.broadcasted_iota(jnp.int32,(W,128),1)
    def slot(s,_):
        r0=offs[0,0,0,s]; c0=offs[0,0,1,s]
        q=c0//128; sh=c0-q*128
        keep=lane<128-sh
        o=[]
        for ch in range(2):
            x=[pltpu.roll(ext[ch,q+j,pl.ds(r0,W),:],128-sh,1) for j in range(3)]
            o.append(jnp.concatenate([jnp.where(keep,x[0],x[1]),jnp.where(keep,x[1],x[2])],axis=1))
        orr,oi=o
        pr=probe[0]; pi=probe[1]
        ar=pr*orr-pi*oi; ai=pr*oi+pi*orr
        ar,ai=right_mul(ar,ai,th,tl,0)
        ar,ai=left_mul(ar,ai,th,tl,0)
        res=ar*ar+ai*ai-mv[s]
        ar,ai=right_mul(res*ar,res*ai,th,tl,1)
        br,bi=left_mul(ar,ai,th,tl,1)
        pg[0]+=orr*br+oi*bi
        pg[1]+=orr*bi-oi*br
        pg[2]+=orr*orr+oi*oi
        gr=pr*br+pi*bi; gi=pr*bi-pi*br
        low=lane<sh
        for ch,g in enumerate((gr,gi)):
            a=pltpu.roll(g[:,:128],sh,1); b=pltpu.roll(g[:,128:],sh,1)
            z=jnp.zeros_like(a)
            grad[ch,q,pl.ds(r0,W),:]+=jnp.where(low,z,a)
            grad[ch,q+1,pl.ds(r0,W),:]+=jnp.where(low,a,b)
            grad[ch,q+2,pl.ds(r0,W),:]+=jnp.where(low,b,z)
        return 0
    lax.fori_loop(0,live[0,0],slot,0)


def compute(offs,live,ext,probe,meas,hi,lo):
    f=jnp.float32
    sd=jax.ShapeDtypeStruct
    V=pl.BlockSpec(memory_space=pltpu.VMEM); M=pl.BlockSpec(memory_space=pltpu.SMEM)
    return pl.pallas_call(kernel,
        out_shape=[sd((2,6,T+W,128),f),sd((3,W,W),f)],
        in_specs=[M,M,V,V,V,V,V],out_specs=[V,V],
        compiler_params=pltpu.CompilerParams(vmem_limit_bytes=VM2*2**20),
    )(jnp.swapaxes(offs,2,3),live,ext,probe,meas,hi,lo)


VM1, VM3 = 4, 16


MESH = pl.DeviceIdType.MESH


def put(src, dst, send, recv, device):
    return pltpu.make_async_remote_copy(src_ref=src, dst_ref=dst, send_sem=send, recv_sem=recv, device_id=device, device_id_type=MESH)


def places():
    row, col = lax.axis_index("row"), lax.axis_index("col")
    rows, cols = lax.axis_size("row"), lax.axis_size("col")
    return row, col, ((row + rows - 1) % rows, col), ((row + 1) % rows, col), (row, (col + cols - 1) % cols), (row, (col + 1) % cols)


def greet(devices):
    barrier = pltpu.get_barrier_semaphore()
    for device in devices:
        pl.semaphore_signal(barrier, inc=1, device_id=device, device_id_type=MESH)
    return barrier


def halo_kernel(tile, probe, meas, th, tl, ext, probev, measv, thv, tlv, hop1, hop2, loc, snd, rcv):
    row, col, up, down, left, right = places()
    loads = []

    def load(src, dst):
        c = pltpu.make_async_copy(src, dst, loc.at[len(loads)])
        loads.append(c)
        c.start()

    barrier = greet((right, up, down))
    pl.semaphore_wait(barrier, 3)
    n = [0]
    sent = []

    def send(src, dst, device):
        k = n[0]
        n[0] += 1
        c = put(src, dst, snd.at[k], rcv.at[k], device)
        c.start()
        sent.append(c)
        return c

    def lanes(cb):
        return pl.ds(128 * cb, 128)

    H = W // 2
    low = pl.ds(T, W)
    far = [pl.ds(T + H * k, H) for k in range(2)]
    first = [send(tile.at[:, pl.ds(H * k, H), lanes(3)], hop1.at[k], down) for k in range(2)]
    b = [send(tile.at[:, pl.ds(0, W), lanes(cb)], ext.at[:, cb, low, :], up) for cb in range(2)]
    r = [send(tile.at[:, :, lanes(cb)], ext.at[:, 4 + cb, pl.ds(0, T), :], left) for cb in range(2)]
    b2 = send(tile.at[:, pl.ds(0, W), lanes(2)], ext.at[:, 2, low, :], up)
    for cb in range(4):
        load(tile.at[:, :, lanes(cb)], ext.at[:, cb, pl.ds(0, T), :])
    for src, dst in ((probe, probev), (meas, measv), (th, thv), (tl, tlv)):
        load(src, dst)
    second, third, x = [], [], []
    for k in range(2):
        first[k].wait_recv()
        second.append(send(hop1.at[k], hop2.at[k], down))
    for k in range(2):
        b[k].wait_recv()
        x.append(send(ext.at[:, k, low, :], ext.at[:, 4 + k, low, :], left))
        second[k].wait_recv()
        third.append(send(hop2.at[k], ext.at[:, 3, far[k], :], down))
    for c in loads:
        c.wait()
    for c in (*r, b2, *third, *x):
        c.wait_recv()
    for c in sent:
        c.wait_send()


def halos(tile, probe, meas, th, tl):
    f = jnp.float32
    A = pl.BlockSpec(memory_space=pl.ANY)
    sd = jax.ShapeDtypeStruct
    H = W // 2
    same = [sd(a.shape, a.dtype) for a in (probe, meas, th, tl)]
    return pl.pallas_call(lambda *a: halo_kernel(*a), out_shape=[sd((2, 6, T + W, 128), f), *same],
        in_specs=[pl.BlockSpec(memory_space=pltpu.HBM)] * 5, out_specs=[A] * 5,
        scratch_shapes=[pltpu.VMEM((2, 2, H, 128), f), pltpu.VMEM((2, 2, H, 128), f), pltpu.SemaphoreType.DMA((8,)), pltpu.SemaphoreType.DMA((13,)), pltpu.SemaphoreType.DMA((13,))],
        compiler_params=pltpu.CompilerParams(collective_id=0, has_side_effects=True, vmem_limit_bytes=VM1*2**20))(tile, probe, meas, th, tl)


def spill_kernel(g, pg, grad, step, gv, rrv, brv, hop1, hop2, zhop1, zhop2, corner, bleft, mine, half, acc, plane, part, ybuf, shard, stepv, loc, snd, rcv, psnd, prcv, gsnd, grcv, zsnd, zrcv):
    row, col, up, down, left, right = places()
    rows, depth = lax.axis_size("row"), 4
    chips = lax.axis_size("col") // 2
    wide = chips // depth
    core, chip = col % 2, col // 2
    x, z = chip // depth, chip % depth
    H = W // 2
    step_rows = H // chips

    def at(xx, zz, cc):
        return (row, ((xx % wide) * depth + zz % depth) * 2 + cc)

    def peer(j):
        return (row, ((chip + j) % chips) * 2 + core)

    sib = at(x, z, 1 - core)
    zm = at(x, z + depth - 1, core)
    around = at(x + jnp.where(z == 1, 1, 0), z + depth - 1, 0)
    source = at(x + jnp.where(z == 0, wide - 1, 0), z + 1, 1)
    ys = [((row + k) % rows, col) for k in range(1, 4)]
    barrier = greet((left, sib, *ys))

    @pl.when(core == 0)
    def _():
        pl.semaphore_signal(barrier, inc=1, device_id=source, device_id_type=MESH)

    def hello(j, _):
        pl.semaphore_signal(barrier, inc=1, device_id=peer(j), device_id_type=MESH)
        return 0

    lax.fori_loop(1, chips, hello, 0)
    loads = []

    def load(src, dst):
        c = pltpu.make_async_copy(src, dst, loc.at[len(loads)])
        loads.append(c)
        c.start()
        return c

    def block(start, size):
        return pl.ds(pl.multiple_of(start, size), size)

    low, top = pl.ds(T, W), pl.ds(0, T)
    l_mine = load(pg.at[:, block(core * H, H), :], mine)
    l_left = load(g.at[:, pl.ds(0, 2), low, :], bleft)
    l_grad = load(g.at[:, pl.ds(0, 4), top, :], gv)
    pl.semaphore_wait(barrier, 5 + chips - 1 + core)
    n = [0]
    sent = []

    def send(src, dst, device):
        k = n[0]
        n[0] += 1
        c = put(src, dst, snd.at[k], rcv.at[k], device)
        c.start()
        sent.append(c)
        return c

    s1 = send(pg.at[:, block((1 - core) * H, H), :], half, sib)
    sc = [send(g.at[:, 4 + cb, low, :], corner.at[:, cb], right) for cb in range(2)]
    far = [pl.ds(H * k, H) for k in range(2)]
    first = [send(g.at[:, 3, pl.ds(T + H * k, H), :], hop1.at[k], up) for k in range(2)]
    b2 = send(g.at[:, 2, low, :], brv.at[:, 2], down)
    zrows = [pl.ds(H * (k + 1), H) for k in range(3)]

    def zcopy(level, k):
        if level == 0:
            return put(g.at[:, 5, zrows[k], :], zhop1.at[k], zsnd.at[k], zrcv.at[k], zm)
        if level == 1:
            return put(zhop1.at[k], zhop2.at[k], zsnd.at[3 + k], zrcv.at[3 + k], zm)
        return put(zhop2.at[k], rrv.at[:, 1, zrows[k], :], zsnd.at[6 + k], zrcv.at[6 + k], around)

    def zdirect(k):
        return put(g.at[:, 5, zrows[k], :], rrv.at[:, 1, zrows[k], :], zsnd.at[k], zrcv.at[6 + k], sib)

    @pl.when(core == 1)
    def _():
        for k in range(3):
            zcopy(0, k).start()

    @pl.when(core == 0)
    def _():
        for k in range(3):
            zdirect(k).start()

    l_mine.wait()
    s1.wait_recv()
    acc[...] = mine[...] + half[...]

    def shard_of(j):
        p = (chip + j) % chips
        return put(acc.at[:, block(p * step_rows, step_rows), :], plane.at[j], psnd.at[j], prcv.at[j], peer(j))

    def begin(j, _):
        shard_of(j).start()
        return 0

    lax.fori_loop(1, chips, begin, 0)
    r = [send(g.at[:, 4, top, :], rrv.at[:, 0], right), send(g.at[:, 5, pl.ds(0, H), :], rrv.at[:, 1, pl.ds(0, H), :], right)]
    l_left.wait()
    b, second, third = [], [], []
    for k in range(2):
        first[k].wait_recv()
        second.append(send(hop1.at[k], hop2.at[k], up))
    for cb in range(2):
        sc[cb].wait_recv()
        bleft[:, cb] += corner[:, cb]
        b.append(send(bleft.at[:, cb], brv.at[:, cb], down))

    @pl.when(core == 1)
    def _():
        for k in range(3):
            zcopy(0, k).wait_recv()
            zcopy(1, k).start()

    part[...] = acc[:, block(chip * step_rows, step_rows), :]

    def collect(j, _):
        shard_of(j).wait_recv()
        part[...] += plane[j]
        return 0

    lax.fori_loop(1, chips, collect, 0)
    yr = [send(part, ybuf.at[row], ys[k]) for k in range(3)]
    ybuf[pl.ds(row, 1)] = part[...][None]
    for k in range(2):
        second[k].wait_recv()
        third.append(send(hop2.at[k], brv.at[:, 3, far[k], :], up))

    @pl.when(core == 1)
    def _():
        for k in range(3):
            zcopy(1, k).wait_recv()
            zcopy(2, k).start()

    for c in yr:
        c.wait_recv()
    total = ybuf[0] + ybuf[1] + ybuf[2] + ybuf[3]
    shard[...] = total[:2] / jnp.sqrt(total[2:])
    here = block(core * H + chip * step_rows, step_rows)

    def gather(j):
        return put(shard, stepv.at[:, here, :], gsnd.at[j], grcv.at[j], peer(j))

    def begin2(j, _):
        gather(j).start()
        return 0

    lax.fori_loop(1, chips, begin2, 0)
    stepv[:, here, :] = shard[...]

    def collect2(j, _):
        gather(j).wait_recv()
        return 0

    lax.fori_loop(1, chips, collect2, 0)
    mine_rows = block(core * H, H)
    s5 = send(stepv.at[:, mine_rows, :], stepv.at[:, mine_rows, :], sib)
    l_grad.wait()
    for c in r:
        c.wait_recv()
    for k in range(3):
        zcopy(2, k).wait_recv()

    def add_left(k, _):
        at_rows = block(k * 32, 32)
        gv[:, :2, at_rows, :] += rrv[:, :, at_rows, :]
        return 0

    lax.fori_loop(0, T // 32, add_left, 0)
    for c in (b2, *b, *third):
        c.wait_recv()

    def add_top(k, _):
        at_rows = block(k * 32, 32)
        gv[:, :, at_rows, :] += brv[:, :, at_rows, :]
        return 0

    lax.fori_loop(0, W // 32, add_top, 0)
    outs = [load(gv.at[:, cb], grad.at[:, :, pl.ds(128 * cb, 128)]) for cb in range(4)]
    s5.wait_recv()
    outs.append(load(stepv, step))

    def drain(j, _):
        shard_of(j).wait_send()
        gather(j).wait_send()
        return 0

    lax.fori_loop(1, chips, drain, 0)
    for c in sent:
        c.wait_send()

    @pl.when(core == 1)
    def _():
        for level in range(3):
            for k in range(3):
                zcopy(level, k).wait_send()

    @pl.when(core == 0)
    def _():
        for k in range(3):
            zdirect(k).wait_send()

    for c in outs:
        c.wait()


def spills(g, pg, rows, cols):
    f = jnp.float32
    A = pl.BlockSpec(memory_space=pl.ANY)
    sd = jax.ShapeDtypeStruct
    V = pltpu.VMEM
    D = pltpu.SemaphoreType.DMA
    H = W // 2
    chips = cols // 2
    sh = H // chips
    return pl.pallas_call(lambda *a: spill_kernel(*a), out_shape=[sd((2, T, T), f), sd((2, W, W), f)],
        in_specs=[A] * 2, out_specs=[A, A],
        scratch_shapes=[V((2, 4, T, 128), f), V((2, 2, T, 128), f), V((2, 4, W, 128), f), V((2, 2, H, 128), f), V((2, 2, H, 128), f),
            V((3, 2, H, 128), f), V((3, 2, H, 128), f), V((2, 2, W, 128), f), V((2, 2, W, 128), f),
            V((3, H, W), f), V((3, H, W), f), V((3, H, W), f), V((chips, 3, sh, W), f), V((3, sh, W), f), V((rows, 3, sh, W), f), V((2, sh, W), f), V((2, W, W), f),
            D((8,)), D((18,)), D((18,)), D((chips,)), D((chips,)), D((chips,)), D((chips,)), D((9,)), D((9,))],
        compiler_params=pltpu.CompilerParams(collective_id=1, has_side_effects=True, vmem_limit_bytes=VM3*2**20))(g, pg)


def local(specimen, probe_field, measured, offsets, live_counts):
    hi, lo = tables()
    ext, probe, meas, hi, lo = halos(specimen, probe_field, measured[0, 0], jnp.asarray(hi), jnp.asarray(lo))
    g, pg = compute(offsets, live_counts, ext, probe, meas, hi, lo)
    grad, step = spills(g, pg, lax.axis_size("row"), lax.axis_size("col"))
    return (grad, step)


def solution(mesh):
    from jax.sharding import PartitionSpec as P
    in_specs = (P(None, "row", "col"), P(), P("row", "col", None, None, None), P("row", "col", None, None), P("row", "col"))
    out_specs = (P(None, "row", "col"), P())
    return jax.shard_map(local, mesh=mesh, in_specs=in_specs, out_specs=out_specs, check_vma=False)
```

time: 93.1 us -> 87.9 us (0.944)
  Pallas kernels: 86.1 us -> 77.8 us
  local copies, waits for them, and re-layouts: 3.61 us -> 8.42 us
  other arithmetic: 1.86 us -> 0 us
    pallas_call x3, Pallas kernels: 86.1 us -> 77.8 us  [the longest x1 48.2 us: spills(): pl.pallas_call(lambda *a: spill_kernel(*a), out_shape=[sd((2, T, T), f),...]
    unnamed x10 -> x14, local copies, waits for them, and re-layouts: 3 us -> 8.42 us
    scatter-add x2 -> x0, other arithmetic: 1.86 us -> none  [local(): grad = G.at[:, :, :W].add(from_left).at[:, :W, :].add(from_above)]
where the time goes in v3:
time: 87.9 us; the launch traced here: 87.6 us
  Pallas kernels  77.8 us (89%)
  local copies, waits for them, and re-layouts  8.42 us (10%)
  between operations  1.32 us (2%)
    pallas_call x1, Pallas kernels, spills(): pl.pallas_call(lambda *a: spill_kernel(*a), out_shape=[sd((2, T, T), f),...  48.2 us
    pallas_call x1, Pallas kernels, halos(): pl.pallas_call(lambda *a: halo_kernel(*a), out_shape=[sd((2, 6, T + W, 12...  24.8 us
    unnamed x14, local copies, waits for them, and re-layouts  8.42 us
    pallas_call x1, Pallas kernels, compute(): pl.pallas_call(kernel, out_shape=[sd((2, 6, T + W, 128), f), sd((3, W, W)...  4.9 us

profile of v3, /device:TPU:1, one launch (start us, length us, event | category | flops | bytes accessed | tf_op | source)
XLA Modules:
  0.0 87.6 jit_solution(8451475458250298158)
XLA Ops:
  1.3 0.0 copy-start
  1.3 1.6 %copy-done = f32[2,512,512]{2,1,0:T(8,128)S(1)} copy-done((f32[2,512,512]{2,1,0:T(8,128)S(1)}, f32[2,512,512]{2,1,0:T(8,128)}, u32[]{:S(2)}) %copy-start) | copy-done | bytes 2097176
  2.9 0.0 copy-start.1
  2.9 1.6 %copy-done.1 = f32[1,1,8,256,256]{4,3,2,1,0:T(8,128)S(1)} copy-done((f32[1,1,8,256,256]{4,3,2,1,0:T(8,128)S(1)}, f32[1,1,8,256,256]{4,3,2,1,0:T(8,128)}, u32[]{:S(2)}) %copy-start.1) | copy-done | bytes 2097176
  4.5 0.0 copy-start.2
  4.5 1.0 %copy-done.2 = f32[2,256,256]{2,1,0:T(8,128)S(1)} copy-done((f32[2,256,256]{2,1,0:T(8,128)S(1)}, f32[2,256,256]{2,1,0:T(8,128)}, u32[]{:S(2)}) %copy-start.2) | copy-done | bytes 524312
  5.5 0.0 copy-start.3
  5.5 1.0 %copy-done.3 = bf16[2,2,256,256]{3,2,1,0:T(8,128)(2,1)S(1)} copy-done((bf16[2,2,256,256]{3,2,1,0:T(8,128)(2,1)S(1)}, bf16[2,2,256,256]{3,2,1,0:T(8,128)(2,1)}, u32[]{:S(2)}) %copy-start.3) | copy-done | bytes 524312
  6.5 0.0 copy-start.4
  6.5 1.0 %copy-done.4 = bf16[2,2,256,256]{3,2,1,0:T(8,128)(2,1)S(1)} copy-done((bf16[2,2,256,256]{3,2,1,0:T(8,128)(2,1)S(1)}, bf16[2,2,256,256]{3,2,1,0:T(8,128)(2,1)}, u32[]{:S(2)}) %copy-start.4) | copy-done | bytes 524312
  7.6 0.0 copy-start.5
  7.6 24.8 %shard_map.86 = (f32[2,6,768,128]{3,2,1,0:T(8,128)S(1)}, f32[2,256,256]{2,1,0:T(8,128)S(1)}, f32[8,256,256]{2,1,0:T(8,128)S(1)}, bf16[2,2,256,256]{3,2,1,0:T(8,128)(2,1)S(1)}, bf16[2,2,256,256]{3,2,1,0:T(8,128)(2,1)S(1)}) custom-call(f32[2,512,512]{2,1,0:T(8,128)S(1)} %copy-done, f32[2,256,256]{2,1,0:T(8,128)S(1)} %copy-done.2, f32[8,256,256]{2,1,0:T(8,128)S(1)} %bitcast.2, ...), custom_call_target="tpu_custom_call" | custom-call | tf_op jit(solution)/shard_map/pallas_call | solution.py:189
  32.4 0.0 copy-done.5
  32.4 4.9 %shard_map.87 = (f32[2,6,768,128]{3,2,1,0:T(8,128)S(1)}, f32[3,256,256]{2,1,0:T(8,128)S(1)}) custom-call(s32[1,1,2,8]{3,2,1,0:T(2,128)S(1)} %bitcast.3, s32[1,1]{1,0:T(1,128)S(6)} %copy.11.live, f32[2,6,768,128]{3,2,1,0:T(8,128)S(1)} %get-tuple-element.9.ext, f32[2,256,256]{2,1,0:T(8,128)S(1)} %get-tuple-element.10.probe, ...), custom_call_target="tpu_custom_call" | custom-call | tf_op jit(solution)/shard_map/pallas_call | solution.py:100
  37.3 48.2 %shard_map.88 = (f32[2,512,512]{2,1,0:T(8,128)S(1)}, f32[2,256,256]{2,1,0:T(8,128)S(1)}) custom-call(f32[2,6,768,128]{3,2,1,0:T(8,128)S(1)} %get-tuple-element.14.a_0_, f32[3,256,256]{2,1,0:T(8,128)S(1)} %get-tuple-element.15.a_1_), custom_call_target="tpu_custom_call" | custom-call | tf_op jit(solution)/shard_map/pallas_call | solution.py:412
  85.5 1.3 %copy.12 = f32[2,512,512]{2,1,0:T(8,128)} copy(f32[2,512,512]{2,1,0:T(8,128)S(1)} %get-tuple-element.18) | data formatting | bytes 4194304
  86.8 0.8 copy.13
Async XLA Ops:
  1.3 1.6 %copy-start = (f32[2,512,512]{2,1,0:T(8,128)S(1)}, f32[2,512,512]{2,1,0:T(8,128)}, u32[]{:S(2)}) copy-start(f32[2,512,512]{2,1,0:T(8,128)} %a_0_.1) | copy-start | bytes 6291460
  2.9 1.6 %copy-start.1 = (f32[1,1,8,256,256]{4,3,2,1,0:T(8,128)S(1)}, f32[1,1,8,256,256]{4,3,2,1,0:T(8,128)}, u32[]{:S(2)}) copy-start(f32[1,1,8,256,256]{4,3,2,1,0:T(8,128)} %param.9) | copy-start | bytes 6291460
  4.5 1.0 %copy-start.2 = (f32[2,256,256]{2,1,0:T(8,128)S(1)}, f32[2,256,256]{2,1,0:T(8,128)}, u32[]{:S(2)}) copy-start(f32[2,256,256]{2,1,0:T(8,128)} %a_1_.1) | copy-start | bytes 1572868
  5.5 1.0 %copy-start.3 = (bf16[2,2,256,256]{3,2,1,0:T(8,128)(2,1)S(1)}, bf16[2,2,256,256]{3,2,1,0:T(8,128)(2,1)}, u32[]{:S(2)}) copy-start(bf16[2,2,256,256]{3,2,1,0:T(8,128)(2,1)} %constant.5.clone.a_4_) | copy-start | bytes 1572868
  6.5 1.0 %copy-start.4 = (bf16[2,2,256,256]{3,2,1,0:T(8,128)(2,1)S(1)}, bf16[2,2,256,256]{3,2,1,0:T(8,128)(2,1)}, u32[]{:S(2)}) copy-start(bf16[2,2,256,256]{3,2,1,0:T(8,128)(2,1)} %constant.4.clone.a_3_) | copy-start | bytes 1572868
  7.6 24.8 %copy-start.5 = (s32[1,1,8,2]{2,3,1,0:T(2,128)S(1)}, s32[1,1,8,2]{2,3,1,0:T(2,128)}, u32[]{:S(2)}) copy-start(s32[1,1,8,2]{2,3,1,0:T(2,128)} %param.10) | copy-start | bytes 196

commit v4 on v3

--- a/solution.py
+++ b/solution.py
@@ -189,7 +189,7 @@
     return pl.pallas_call(lambda *a: halo_kernel(*a), out_shape=[sd((2, 6, T + W, 128), f), *same],
         in_specs=[pl.BlockSpec(memory_space=pltpu.HBM)] * 5, out_specs=[A] * 5,
         scratch_shapes=[pltpu.VMEM((2, 2, H, 128), f), pltpu.VMEM((2, 2, H, 128), f), pltpu.SemaphoreType.DMA((8,)), pltpu.SemaphoreType.DMA((13,)), pltpu.SemaphoreType.DMA((13,))],
-        compiler_params=pltpu.CompilerParams(collective_id=0, has_side_effects=True, vmem_limit_bytes=VM1*2**20))(tile, probe, meas, th, tl)
+        compiler_params=pltpu.CompilerParams(collective_id=0, has_side_effects=True, vmem_limit_bytes=VM1*2**20))(*[pltpu.with_memory_space_constraint(a, pltpu.HBM) for a in (tile, probe, meas, th, tl)])
 
 
 def spill_kernel(g, pg, grad, step, gv, rrv, brv, hop1, hop2, zhop1, zhop2, corner, bleft, mine, half, acc, plane, part, ybuf, shard, stepv, loc, snd, rcv, psnd, prcv, gsnd, grcv, zsnd, zrcv):

time: 87.9 us -> 80.7 us (0.918)
  local copies, waits for them, and re-layouts: 8.42 us -> 2.12 us
    unnamed x14 -> x4, local copies, waits for them, and re-layouts: 8.42 us -> 2.12 us
    pallas_call x1, Pallas kernels: 48.2 us -> 47.1 us  [spills(): pl.pallas_call(lambda *a: spill_kernel(*a), out_shape=[sd((2, T, T), f),...]
where the time goes in v4:
time: 80.7 us; the launch traced here: 80.6 us
  Pallas kernels  77.1 us (96%)
  local copies, waits for them, and re-layouts  2.12 us (3%)
  between operations  1.32 us (2%)
    pallas_call x1, Pallas kernels, spills(): pl.pallas_call(lambda *a: spill_kernel(*a), out_shape=[sd((2, T, T), f),...  47.1 us
    pallas_call x1, Pallas kernels, halos(): pl.pallas_call(lambda *a: halo_kernel(*a), out_shape=[sd((2, 6, T + W, 12...  25.1 us
    pallas_call x1, Pallas kernels, compute(): pl.pallas_call(kernel, out_shape=[sd((2, 6, T + W, 128), f), sd((3, W, W)...  4.88 us
    unnamed x4, local copies, waits for them, and re-layouts  2.12 us

profile of v4, /device:TPU:1, one launch (start us, length us, event | category | flops | bytes accessed | tf_op | source)
XLA Modules:
  0.0 80.6 jit_solution(10487367628036046285)
XLA Ops:
  1.3 0.0 copy-start
  1.3 25.1 %shard_map.86 = (f32[2,6,768,128]{3,2,1,0:T(8,128)S(1)}, f32[2,256,256]{2,1,0:T(8,128)S(1)}, f32[8,256,256]{2,1,0:T(8,128)S(1)}, bf16[2,2,256,256]{3,2,1,0:T(8,128)(2,1)S(1)}, bf16[2,2,256,256]{3,2,1,0:T(8,128)(2,1)S(1)}) custom-call(f32[2,512,512]{2,1,0:T(8,128)} %a_0_.1, f32[2,256,256]{2,1,0:T(8,128)} %a_1_.1, f32[8,256,256]{2,1,0:T(8,128)} %bitcast.3, ...), custom_call_target="tpu_custom_call" | custom-call | tf_op jit(solution)/shard_map/pallas_call | solution.py:189
  26.4 0.0 copy-done
  26.4 4.9 %shard_map.87 = (f32[2,6,768,128]{3,2,1,0:T(8,128)S(1)}, f32[3,256,256]{2,1,0:T(8,128)S(1)}) custom-call(s32[1,1,2,8]{3,2,1,0:T(2,128)S(1)} %bitcast.2, s32[1,1]{1,0:T(1,128)S(6)} %copy.11.live, f32[2,6,768,128]{3,2,1,0:T(8,128)S(1)} %get-tuple-element.9.ext, f32[2,256,256]{2,1,0:T(8,128)S(1)} %get-tuple-element.10.probe, ...), custom_call_target="tpu_custom_call" | custom-call | tf_op jit(solution)/shard_map/pallas_call | solution.py:100
  31.3 47.1 %shard_map.88 = (f32[2,512,512]{2,1,0:T(8,128)S(1)}, f32[2,256,256]{2,1,0:T(8,128)S(1)}) custom-call(f32[2,6,768,128]{3,2,1,0:T(8,128)S(1)} %get-tuple-element.14.a_0_, f32[3,256,256]{2,1,0:T(8,128)S(1)} %get-tuple-element.15.a_1_), custom_call_target="tpu_custom_call" | custom-call | tf_op jit(solution)/shard_map/pallas_call | solution.py:412
  78.5 1.3 %copy.12 = f32[2,512,512]{2,1,0:T(8,128)} copy(f32[2,512,512]{2,1,0:T(8,128)S(1)} %get-tuple-element.18) | data formatting | bytes 4194304
  79.8 0.8 copy.13
Async XLA Ops:
  1.3 25.1 %copy-start = (s32[1,1,8,2]{2,3,1,0:T(2,128)S(1)}, s32[1,1,8,2]{2,3,1,0:T(2,128)}, u32[]{:S(2)}) copy-start(s32[1,1,8,2]{2,3,1,0:T(2,128)} %param.10) | copy-start | bytes 196

commit v5 on v4

--- a/solution.py
+++ b/solution.py
@@ -62,7 +62,7 @@
     grad[...]=jnp.zeros_like(grad)
     pg[...]=jnp.zeros_like(pg)
     lane=lax.broadcasted_iota(jnp.int32,(W,128),1)
-    def slot(s,_):
+    def open_slot(s,on):
         r0=offs[0,0,0,s]; c0=offs[0,0,1,s]
         q=c0//128; sh=c0-q*128
         keep=lane<128-sh
@@ -72,15 +72,21 @@
             o.append(jnp.concatenate([jnp.where(keep,x[0],x[1]),jnp.where(keep,x[1],x[2])],axis=1))
         orr,oi=o
         pr=probe[0]; pi=probe[1]
-        ar=pr*orr-pi*oi; ai=pr*oi+pi*orr
-        ar,ai=right_mul(ar,ai,th,tl,0)
-        ar,ai=left_mul(ar,ai,th,tl,0)
-        res=ar*ar+ai*ai-mv[s]
-        ar,ai=right_mul(res*ar,res*ai,th,tl,1)
-        br,bi=left_mul(ar,ai,th,tl,1)
+        return (s,on,r0,q,sh,orr,oi),(pr*orr-pi*oi,pr*oi+pi*orr)
+    def middle(st,a):
+        ar,ai=a
+        s,on=st[:2]
+        res=(ar*ar+ai*ai-mv[s])
+        if on is not None: res=res*on
+        return res*ar,res*ai
+    def close_slot(st,a):
+        s,on,r0,q,sh,orr,oi=st
+        br,bi=a
+        pr=probe[0]; pi=probe[1]
         pg[0]+=orr*br+oi*bi
         pg[1]+=orr*bi-oi*br
-        pg[2]+=orr*orr+oi*oi
+        il=orr*orr+oi*oi
+        pg[2]+=il if on is None else il*on
         gr=pr*br+pi*bi; gi=pr*bi-pi*br
         low=lane<sh
         for ch,g in enumerate((gr,gi)):
@@ -89,9 +95,17 @@
             grad[ch,q,pl.ds(r0,W),:]+=jnp.where(low,z,a)
             grad[ch,q+1,pl.ds(r0,W),:]+=jnp.where(low,a,b)
             grad[ch,q+2,pl.ds(r0,W),:]+=jnp.where(low,b,z)
-        return 0
-    lax.fori_loop(0,live[0,0],slot,0)
-
+    def pair(p,_):
+        on=(2*p+1<live[0,0]).astype(jnp.float32)
+        sts,vs=zip(*[open_slot(2*p,None),open_slot(2*p+1,on)])
+        vs=[right_mul(*v,th,tl,0) for v in vs]
+        vs=[left_mul(*v,th,tl,0) for v in vs]
+        vs=[middle(st,v) for st,v in zip(sts,vs)]
+        vs=[right_mul(*v,th,tl,1) for v in vs]
+        vs=[left_mul(*v,th,tl,1) for v in vs]
+        for st,v in zip(sts,vs): close_slot(st,v)
+        return 0
+    lax.fori_loop(0,(live[0,0]+1)//2,pair,0)
 
 def compute(offs,live,ext,probe,meas,hi,lo):
     f=jnp.float32
@@ -104,7 +118,7 @@
     )(jnp.swapaxes(offs,2,3),live,ext,probe,meas,hi,lo)
 
 
-VM1, VM3 = 4, 16
+VM1, VM3, NC = 4, 16, 64
 
 
 MESH = pl.DeviceIdType.MESH
@@ -192,6 +206,9 @@
         compiler_params=pltpu.CompilerParams(collective_id=0, has_side_effects=True, vmem_limit_bytes=VM1*2**20))(*[pltpu.with_memory_space_constraint(a, pltpu.HBM) for a in (tile, probe, meas, th, tl)])
 
 
+GIVE = ((0, 1), (2,), (3,))
+
+
 def spill_kernel(g, pg, grad, step, gv, rrv, brv, hop1, hop2, zhop1, zhop2, corner, bleft, mine, half, acc, plane, part, ybuf, shard, stepv, loc, snd, rcv, psnd, prcv, gsnd, grcv, zsnd, zrcv):
     row, col, up, down, left, right = places()
     rows, depth = lax.axis_size("row"), 4
@@ -252,7 +269,8 @@
         return c
 
     s1 = send(pg.at[:, block((1 - core) * H, H), :], half, sib)
-    sc = [send(g.at[:, 4 + cb, low, :], corner.at[:, cb], right) for cb in range(2)]
+    cuts = [pl.ds(NC * k, NC) for k in range(W // NC)]
+    sc = [send(g.at[:, 4:6, pl.ds(T + NC * k, NC), :], corner.at[:, :, cuts[k], :], right) for k in range(W // NC)]
     far = [pl.ds(H * k, H) for k in range(2)]
     first = [send(g.at[:, 3, pl.ds(T + H * k, H), :], hop1.at[k], up) for k in range(2)]
     b2 = send(g.at[:, 2, low, :], brv.at[:, 2], down)
@@ -294,13 +312,16 @@
     r = [send(g.at[:, 4, top, :], rrv.at[:, 0], right), send(g.at[:, 5, pl.ds(0, H), :], rrv.at[:, 1, pl.ds(0, H), :], right)]
     l_left.wait()
     b, second, third = [], [], []
-    for k in range(2):
-        first[k].wait_recv()
-        second.append(send(hop1.at[k], hop2.at[k], up))
-    for cb in range(2):
-        sc[cb].wait_recv()
-        bleft[:, cb] += corner[:, cb]
-        b.append(send(bleft.at[:, cb], brv.at[:, cb], down))
+    def give(k):
+        sc[k].wait_recv()
+        bleft[:, :, cuts[k], :] += corner[:, :, cuts[k], :]
+        b.append(send(bleft.at[:, :, cuts[k], :], brv.at[:, 0:2, cuts[k], :], down))
+
+    for k in GIVE[0]:
+        give(k)
+    for j in range(2):
+        first[j].wait_recv()
+        second.append(send(hop1.at[j], hop2.at[j], up))
 
     @pl.when(core == 1)
     def _():
@@ -318,16 +339,8 @@
     lax.fori_loop(1, chips, collect, 0)
     yr = [send(part, ybuf.at[row], ys[k]) for k in range(3)]
     ybuf[pl.ds(row, 1)] = part[...][None]
-    for k in range(2):
-        second[k].wait_recv()
-        third.append(send(hop2.at[k], brv.at[:, 3, far[k], :], up))
-
-    @pl.when(core == 1)
-    def _():
-        for k in range(3):
-            zcopy(1, k).wait_recv()
-            zcopy(2, k).start()
-
+    for k in GIVE[1]:
+        give(k)
     for c in yr:
         c.wait_recv()
     total = ybuf[0] + ybuf[1] + ybuf[2] + ybuf[3]
@@ -343,6 +356,18 @@
 
     lax.fori_loop(1, chips, begin2, 0)
     stepv[:, here, :] = shard[...]
+    for k in GIVE[2]:
+        give(k)
+    for k in range(2):
+        second[k].wait_recv()
+        third.append(send(hop2.at[k], brv.at[:, 3, far[k], :], up))
+
+    @pl.when(core == 1)
+    def _():
+        for k in range(3):
+            zcopy(1, k).wait_recv()
+            zcopy(2, k).start()
+
 
     def collect2(j, _):
         gather(j).wait_recv()
@@ -414,7 +439,7 @@
         scratch_shapes=[V((2, 4, T, 128), f), V((2, 2, T, 128), f), V((2, 4, W, 128), f), V((2, 2, H, 128), f), V((2, 2, H, 128), f),
             V((3, 2, H, 128), f), V((3, 2, H, 128), f), V((2, 2, W, 128), f), V((2, 2, W, 128), f),
             V((3, H, W), f), V((3, H, W), f), V((3, H, W), f), V((chips, 3, sh, W), f), V((3, sh, W), f), V((rows, 3, sh, W), f), V((2, sh, W), f), V((2, W, W), f),
-            D((8,)), D((18,)), D((18,)), D((chips,)), D((chips,)), D((chips,)), D((chips,)), D((9,)), D((9,))],
+            D((8,)), D((40,)), D((40,)), D((chips,)), D((chips,)), D((chips,)), D((chips,)), D((9,)), D((9,))],
         compiler_params=pltpu.CompilerParams(collective_id=1, has_side_effects=True, vmem_limit_bytes=VM3*2**20))(g, pg)
 
 

time: 80.7 us -> 70.8 us (0.88)
  Pallas kernels: 77.1 us -> 67.2 us
    pallas_call x1, Pallas kernels: 47.1 us -> 38.6 us  [spills(): pl.pallas_call(lambda *a: spill_kernel(*a), out_shape=[sd((2, T, T), f),...]
    pallas_call x1, Pallas kernels: 4.88 us -> 3.48 us  [compute(): pl.pallas_call(kernel, out_shape=[sd((2, 6, T + W, 128), f), sd((3, W, W)...]
where the time goes in v5:
time: 70.8 us; the launch traced here: 70.6 us
  Pallas kernels  67.2 us (95%)
  local copies, waits for them, and re-layouts  2.12 us (3%)
  between operations  1.32 us (2%)
    pallas_call x1, Pallas kernels, spills(): pl.pallas_call(lambda *a: spill_kernel(*a), out_shape=[sd((2, T, T), f),...  38.6 us
    pallas_call x1, Pallas kernels, halos(): pl.pallas_call(lambda *a: halo_kernel(*a), out_shape=[sd((2, 6, T + W, 12...  25.1 us
    pallas_call x1, Pallas kernels, compute(): pl.pallas_call(kernel, out_shape=[sd((2, 6, T + W, 128), f), sd((3, W, W)...  3.48 us
    unnamed x4, local copies, waits for them, and re-layouts  2.12 us

profile of v5, /device:TPU:1, one launch (start us, length us, event | category | flops | bytes accessed | tf_op | source)
XLA Modules:
  0.0 70.6 jit_solution(10138569612806023694)
XLA Ops:
  1.3 0.0 copy-start
  1.3 25.1 %shard_map.86 = (f32[2,6,768,128]{3,2,1,0:T(8,128)S(1)}, f32[2,256,256]{2,1,0:T(8,128)S(1)}, f32[8,256,256]{2,1,0:T(8,128)S(1)}, bf16[2,2,256,256]{3,2,1,0:T(8,128)(2,1)S(1)}, bf16[2,2,256,256]{3,2,1,0:T(8,128)(2,1)S(1)}) custom-call(f32[2,512,512]{2,1,0:T(8,128)} %a_0_.1, f32[2,256,256]{2,1,0:T(8,128)} %a_1_.1, f32[8,256,256]{2,1,0:T(8,128)} %bitcast.3, ...), custom_call_target="tpu_custom_call" | custom-call | tf_op jit(solution)/shard_map/pallas_call | solution.py:203
  26.4 0.0 copy-done
  26.4 3.5 %shard_map.87 = (f32[2,6,768,128]{3,2,1,0:T(8,128)S(1)}, f32[3,256,256]{2,1,0:T(8,128)S(1)}) custom-call(s32[1,1,2,8]{3,2,1,0:T(2,128)S(1)} %bitcast.2, s32[1,1]{1,0:T(1,128)S(6)} %copy.11.live, f32[2,6,768,128]{3,2,1,0:T(8,128)S(1)} %get-tuple-element.9.ext, f32[2,256,256]{2,1,0:T(8,128)S(1)} %get-tuple-element.10.probe, ...), custom_call_target="tpu_custom_call" | custom-call | tf_op jit(solution)/shard_map/pallas_call | solution.py:114
  29.9 38.6 %shard_map.88 = (f32[2,512,512]{2,1,0:T(8,128)S(1)}, f32[2,256,256]{2,1,0:T(8,128)S(1)}) custom-call(f32[2,6,768,128]{3,2,1,0:T(8,128)S(1)} %get-tuple-element.14.a_0_, f32[3,256,256]{2,1,0:T(8,128)S(1)} %get-tuple-element.15.a_1_), custom_call_target="tpu_custom_call" | custom-call | tf_op jit(solution)/shard_map/pallas_call | solution.py:437
  68.5 1.3 %copy.12 = f32[2,512,512]{2,1,0:T(8,128)} copy(f32[2,512,512]{2,1,0:T(8,128)S(1)} %get-tuple-element.18) | data formatting | bytes 4194304
  69.8 0.8 %copy.13 = f32[2,256,256]{2,1,0:T(8,128)} copy(f32[2,256,256]{2,1,0:T(8,128)S(1)} %get-tuple-element.19) | data formatting | bytes 1048576
Async XLA Ops:
  1.3 25.1 %copy-start = (s32[1,1,8,2]{2,3,1,0:T(2,128)S(1)}, s32[1,1,8,2]{2,3,1,0:T(2,128)}, u32[]{:S(2)}) copy-start(s32[1,1,8,2]{2,3,1,0:T(2,128)} %param.10) | copy-start | bytes 196

commit v6 on v5

--- a/solution.py
+++ b/solution.py
@@ -209,7 +209,7 @@
 GIVE = ((0, 1), (2,), (3,))
 
 
-def spill_kernel(g, pg, grad, step, gv, rrv, brv, hop1, hop2, zhop1, zhop2, corner, bleft, mine, half, acc, plane, part, ybuf, shard, stepv, loc, snd, rcv, psnd, prcv, gsnd, grcv, zsnd, zrcv):
+def spill_kernel(g, pg, rrv, brv, step, hop1, hop2, zhop1, zhop2, corner, bleft, mine, half, acc, plane, part, ybuf, shard, loc, snd, rcv, psnd, prcv, gsnd, grcv, fsnd, frcv, zsnd, zrcv):
     row, col, up, down, left, right = places()
     rows, depth = lax.axis_size("row"), 4
     chips = lax.axis_size("col") // 2
@@ -255,7 +255,6 @@
     low, top = pl.ds(T, W), pl.ds(0, T)
     l_mine = load(pg.at[:, block(core * H, H), :], mine)
     l_left = load(g.at[:, pl.ds(0, 2), low, :], bleft)
-    l_grad = load(g.at[:, pl.ds(0, 4), top, :], gv)
     pl.semaphore_wait(barrier, 5 + chips - 1 + core)
     n = [0]
     sent = []
@@ -286,16 +285,6 @@
     def zdirect(k):
         return put(g.at[:, 5, zrows[k], :], rrv.at[:, 1, zrows[k], :], zsnd.at[k], zrcv.at[6 + k], sib)
 
-    @pl.when(core == 1)
-    def _():
-        for k in range(3):
-            zcopy(0, k).start()
-
-    @pl.when(core == 0)
-    def _():
-        for k in range(3):
-            zdirect(k).start()
-
     l_mine.wait()
     s1.wait_recv()
     acc[...] = mine[...] + half[...]
@@ -309,6 +298,16 @@
         return 0
 
     lax.fori_loop(1, chips, begin, 0)
+    @pl.when(core == 1)
+    def _():
+        for k in range(3):
+            zcopy(0, k).start()
+
+    @pl.when(core == 0)
+    def _():
+        for k in range(3):
+            zdirect(k).start()
+
     r = [send(g.at[:, 4, top, :], rrv.at[:, 0], right), send(g.at[:, 5, pl.ds(0, H), :], rrv.at[:, 1, pl.ds(0, H), :], right)]
     l_left.wait()
     b, second, third = [], [], []
@@ -347,15 +346,23 @@
     shard[...] = total[:2] / jnp.sqrt(total[2:])
     here = block(core * H + chip * step_rows, step_rows)
 
+    own = load(shard, step.at[:, here, :])
+
     def gather(j):
-        return put(shard, stepv.at[:, here, :], gsnd.at[j], grcv.at[j], peer(j))
+        return put(shard, step.at[:, here, :], gsnd.at[j], grcv.at[j], peer(j))
 
     def begin2(j, _):
         gather(j).start()
         return 0
 
     lax.fori_loop(1, chips, begin2, 0)
-    stepv[:, here, :] = shard[...]
+
+    def pass_on(j):
+        rows_j = block(core * H + (chip + chips - j) % chips * step_rows, step_rows)
+        return put(step.at[:, rows_j, :], step.at[:, rows_j, :], fsnd.at[j], frcv.at[j], sib)
+
+    own.wait()
+    pass_on(0).start()
     for k in GIVE[2]:
         give(k)
     for k in range(2):
@@ -371,35 +378,21 @@
 
     def collect2(j, _):
         gather(j).wait_recv()
+        pass_on(j).start()
         return 0
 
     lax.fori_loop(1, chips, collect2, 0)
-    mine_rows = block(core * H, H)
-    s5 = send(stepv.at[:, mine_rows, :], stepv.at[:, mine_rows, :], sib)
-    l_grad.wait()
-    for c in r:
+    for c in (*r, b2, *b, *third):
         c.wait_recv()
     for k in range(3):
         zcopy(2, k).wait_recv()
 
-    def add_left(k, _):
-        at_rows = block(k * 32, 32)
-        gv[:, :2, at_rows, :] += rrv[:, :, at_rows, :]
-        return 0
-
-    lax.fori_loop(0, T // 32, add_left, 0)
-    for c in (b2, *b, *third):
-        c.wait_recv()
-
-    def add_top(k, _):
-        at_rows = block(k * 32, 32)
-        gv[:, :, at_rows, :] += brv[:, :, at_rows, :]
-        return 0
-
-    lax.fori_loop(0, W // 32, add_top, 0)
-    outs = [load(gv.at[:, cb], grad.at[:, :, pl.ds(128 * cb, 128)]) for cb in range(4)]
-    s5.wait_recv()
-    outs.append(load(stepv, step))
+    def collect3(j, _):
+        pass_on(j).wait_recv()
+        pass_on(j).wait_send()
+        return 0
+
+    lax.fori_loop(0, chips, collect3, 0)
 
     def drain(j, _):
         shard_of(j).wait_send()
@@ -420,9 +413,6 @@
     def _():
         for k in range(3):
             zdirect(k).wait_send()
-
-    for c in outs:
-        c.wait()
 
 
 def spills(g, pg, rows, cols):
@@ -434,21 +424,50 @@
     H = W // 2
     chips = cols // 2
     sh = H // chips
-    return pl.pallas_call(lambda *a: spill_kernel(*a), out_shape=[sd((2, T, T), f), sd((2, W, W), f)],
-        in_specs=[A] * 2, out_specs=[A, A],
-        scratch_shapes=[V((2, 4, T, 128), f), V((2, 2, T, 128), f), V((2, 4, W, 128), f), V((2, 2, H, 128), f), V((2, 2, H, 128), f),
-            V((3, 2, H, 128), f), V((3, 2, H, 128), f), V((2, 2, W, 128), f), V((2, 2, W, 128), f),
-            V((3, H, W), f), V((3, H, W), f), V((3, H, W), f), V((chips, 3, sh, W), f), V((3, sh, W), f), V((rows, 3, sh, W), f), V((2, sh, W), f), V((2, W, W), f),
-            D((8,)), D((40,)), D((40,)), D((chips,)), D((chips,)), D((chips,)), D((chips,)), D((9,)), D((9,))],
+    return pl.pallas_call(lambda *a: spill_kernel(*a), out_shape=[sd((2, 2, T, 128), f), sd((2, 4, W, 128), f), sd((2, W, W), f)],
+        in_specs=[A] * 2, out_specs=[A] * 3,
+        scratch_shapes=[V((2, 2, H, 128), f), V((2, 2, H, 128), f), V((3, 2, H, 128), f), V((3, 2, H, 128), f), V((2, 2, W, 128), f), V((2, 2, W, 128), f),
+            V((3, H, W), f), V((3, H, W), f), V((3, H, W), f), V((chips, 3, sh, W), f), V((3, sh, W), f), V((rows, 3, sh, W), f), V((2, sh, W), f),
+            D((4,)), D((40,)), D((40,)), *[D((chips,))] * 6, D((9,)), D((9,))],
         compiler_params=pltpu.CompilerParams(collective_id=1, has_side_effects=True, vmem_limit_bytes=VM3*2**20))(g, pg)
+
+
+def join_kernel(g, rrv, brv, stepv, grad, step, out, sem):
+    s = pltpu.make_async_copy(stepv, step, sem.at[4])
+    s.start()
+    cps = []
+    for cb in (3, 2, 1, 0):
+        for k in range(4):
+            at_rows = pl.ds(128 * k, 128)
+            v = g[:, cb, at_rows, :]
+            if cb < 2:
+                v = v + rrv[:, cb, at_rows, :]
+            if k < 2:
+                v = v + brv[:, cb, at_rows, :]
+            out[:, cb, at_rows, :] = v
+        cps.append(pltpu.make_async_copy(out.at[:, cb], grad.at[:, :, pl.ds(128 * cb, 128)], sem.at[cb]))
+        cps[-1].start()
+    for c in (s, *cps):
+        c.wait()
+
+
+def join(g, rrv, brv, stepv):
+    f = jnp.float32
+    V = pl.BlockSpec(memory_space=pltpu.VMEM)
+    A = pl.BlockSpec(memory_space=pl.ANY)
+    sd = jax.ShapeDtypeStruct
+    return pl.pallas_call(join_kernel, out_shape=[sd((2, T, T), f), sd((2, W, W), f)],
+        in_specs=[V, V, V, V], out_specs=[A, A],
+        scratch_shapes=[pltpu.VMEM((2, 4, T, 128), f), pltpu.SemaphoreType.DMA((5,))],
+        compiler_params=pltpu.CompilerParams(vmem_limit_bytes=16*2**20))(g, rrv, brv, stepv)
 
 
 def local(specimen, probe_field, measured, offsets, live_counts):
     hi, lo = tables()
     ext, probe, meas, hi, lo = halos(specimen, probe_field, measured[0, 0], jnp.asarray(hi), jnp.asarray(lo))
     g, pg = compute(offsets, live_counts, ext, probe, meas, hi, lo)
-    grad, step = spills(g, pg, lax.axis_size("row"), lax.axis_size("col"))
-    return (grad, step)
+    rrv, brv, step = spills(g, pg, lax.axis_size("row"), lax.axis_size("col"))
+    return tuple(join(g, rrv, brv, step))
 
 
 def solution(mesh):

time: 70.8 us -> 72.4 us (1.023)
  Pallas kernels: 67.2 us -> 71 us
  local copies, waits for them, and re-layouts: 2.12 us -> 0.01 us
    pallas_call x1, Pallas kernels: 3.48 us -> 11.2 us  [compute(): pl.pallas_call(kernel, out_shape=[sd((2, 6, T + W, 128), f), sd((3, W, W)...]
    pallas_call x1 -> x2, Pallas kernels: 38.6 us -> 34.7 us  [the longest x1 33.2 us: spills(): pl.pallas_call(lambda *a: spill_kernel(*a), out_shape=[sd((2, 2, T, 128),...]
    unnamed x4 -> x2, local copies, waits for them, and re-layouts: 2.12 us -> 0.01 us
where the time goes in v6:
time: 72.4 us; the launch traced here: 72.3 us
  Pallas kernels  71 us (98%)
  between operations  1.32 us (2%)
    pallas_call x1, Pallas kernels, spills(): pl.pallas_call(lambda *a: spill_kernel(*a), out_shape=[sd((2, 2, T, 128),...  33.2 us
    pallas_call x1, Pallas kernels, halos(): pl.pallas_call(lambda *a: halo_kernel(*a), out_shape=[sd((2, 6, T + W, 12...  25.1 us
    pallas_call x1, Pallas kernels, compute(): pl.pallas_call(kernel, out_shape=[sd((2, 6, T + W, 128), f), sd((3, W, W)...  11.2 us
    pallas_call x1, Pallas kernels, join(): pl.pallas_call(join_kernel, out_shape=[sd((2, T, T), f), sd((2, W, W), f)...  1.53 us

profile of v6, /device:TPU:1, one launch (start us, length us, event | category | flops | bytes accessed | tf_op | source)
XLA Modules:
  0.0 72.3 jit_solution(5350493979045241586)
XLA Ops:
  1.3 0.0 copy-start
  1.3 25.1 %shard_map.86 = (f32[2,6,768,128]{3,2,1,0:T(8,128)S(1)}, f32[2,256,256]{2,1,0:T(8,128)S(1)}, f32[8,256,256]{2,1,0:T(8,128)S(1)}, bf16[2,2,256,256]{3,2,1,0:T(8,128)(2,1)S(1)}, bf16[2,2,256,256]{3,2,1,0:T(8,128)(2,1)S(1)}) custom-call(f32[2,512,512]{2,1,0:T(8,128)} %a_0_.1, f32[2,256,256]{2,1,0:T(8,128)} %a_1_.1, f32[8,256,256]{2,1,0:T(8,128)} %bitcast.3, ...), custom_call_target="tpu_custom_call" | custom-call | tf_op jit(solution)/shard_map/pallas_call | solution.py:203
  26.4 0.0 copy-done
  26.4 11.2 %shard_map.87 = (f32[2,6,768,128]{3,2,1,0:T(8,128)S(1)}, f32[3,256,256]{2,1,0:T(8,128)S(1)}) custom-call(s32[1,1,2,8]{3,2,1,0:T(2,128)S(1)} %bitcast.2, s32[1,1]{1,0:T(1,128)S(6)} %copy.9.live, f32[2,6,768,128]{3,2,1,0:T(8,128)S(1)} %get-tuple-element.12.ext, f32[2,256,256]{2,1,0:T(8,128)S(1)} %get-tuple-element.13.probe, ...), custom_call_target="tpu_custom_call" | custom-call | tf_op jit(solution)/shard_map/pallas_call | solution.py:114
  37.6 33.2 %shard_map.88 = (f32[2,2,512,128]{3,2,1,0:T(8,128)S(1)}, f32[2,4,256,128]{3,2,1,0:T(8,128)S(1)}, f32[2,256,256]{2,1,0:T(8,128)S(1)}) custom-call(f32[2,6,768,128]{3,2,1,0:T(8,128)S(1)} %get-tuple-element.17.a_0_.g, f32[3,256,256]{2,1,0:T(8,128)S(1)} %get-tuple-element.18.a_1_), custom_call_target="tpu_custom_call" | custom-call | tf_op jit(solution)/shard_map/pallas_call | solution.py:427
  70.8 1.5 %shard_map.89 = (f32[2,512,512]{2,1,0:T(8,128)}, f32[2,256,256]{2,1,0:T(8,128)}) custom-call(f32[2,6,768,128]{3,2,1,0:T(8,128)S(1)} %get-tuple-element.17.a_0_.g, f32[2,2,512,128]{3,2,1,0:T(8,128)S(1)} %get-tuple-element.19.rrv, f32[2,4,256,128]{3,2,1,0:T(8,128)S(1)} %get-tuple-element.20.brv, f32[2,256,256]{2,1,0:T(8,128)S(1)} %get-tuple-element.21.stepv), custom_call_target="tpu_custom_call" | custom-call | tf_op jit(solution)/shard_map/pallas_call | solution.py:459
Async XLA Ops:
  1.3 25.1 %copy-start = (s32[1,1,8,2]{2,3,1,0:T(2,128)S(1)}, s32[1,1,8,2]{2,3,1,0:T(2,128)}, u32[]{:S(2)}) copy-start(s32[1,1,8,2]{2,3,1,0:T(2,128)} %param.10) | copy-start | bytes 196

commit v7 on v6

--- a/solution.py
+++ b/solution.py
@@ -6,6 +6,7 @@
 
 W=256; T=512; S=8
 VM2=24
+R=32
 BF=jnp.bfloat16
 def tables():
     k=np.arange(W); k=np.where(k<W//2,k,k-W).astype(np.float64)
@@ -58,64 +59,103 @@
     yi=jnp.concatenate([u[H:]+v[H:],u[H:]-v[H:]],axis=0)
     return yr,yi
 
-def kernel(offs,live,ext,probe,mv,th,tl, grad,pg):
-    grad[...]=jnp.zeros_like(grad)
-    pg[...]=jnp.zeros_like(pg)
-    lane=lax.broadcasted_iota(jnp.int32,(W,128),1)
-    def open_slot(s,on):
+def kernel(offs,live,ext,probe,mv,th,tl,g0,pg0, grad,pg,win):
+    H=W//2
+    def dd(a,b): return jnp.dot(a,b,preferred_element_type=jnp.float32)
+    def cols(r,i):
+        return [split(jnp.concatenate([f(r[:,:H],r[:,H:]),f(i[:,:H],i[:,H:])],axis=1)) for f in (jnp.add,jnp.subtract)]
+    def stack(parts): return jnp.concatenate(parts,axis=0)
+    def right(parts,which):
+        out=[]
+        for n in range(2):
+            hi=stack([p[n][0] for p in parts]); lo=stack([p[n][1] for p in parts])
+            p=dd(jnp.concatenate([hi,lo],axis=0),th[1-which,n])
+            out.append(p[:W]+p[W:]+dd(hi,tl[1-which,n]))
+        return out
+    def left(uv,which):
+        u,v=uv
+        re=[[],[]]; im=[[],[]]
+        for c in range(0,H,R):
+            def y(r):
+                a=u[r:r+R]; b=v[r:r+R]
+                p=a+b; m=a-b
+                return jnp.concatenate([p[:,:H],m[:,:H]],axis=1),jnp.concatenate([p[:,H:],m[:,H:]],axis=1)
+            (tr,ti),(br,bi)=y(c),y(c+H)
+            for n,f in enumerate((jnp.add,jnp.subtract)):
+                re[n].append(split(f(tr,br))); im[n].append(split(f(ti,bi)))
+        out=[]
+        for n in range(2):
+            hi=stack([p[0] for p in re[n]]+[p[0] for p in im[n]]); lo=stack([p[1] for p in re[n]]+[p[1] for p in im[n]])
+            p=dd(jnp.concatenate([th[which,n],tl[which,n]],axis=0),hi)
+            out.append(p[:W]+p[W:]+dd(th[which,n],lo))
+        return out
+    def rows(uv):
+        u,v=uv
+        for c in range(0,H,R):
+            ur,ui,vr,vi=u[c:c+R],u[H+c:H+c+R],v[c:c+R],v[H+c:H+c+R]
+            yield c,ur+vr,ui+vi
+            yield c+H,ur-vr,ui-vi
+    def place(s):
         r0=offs[0,0,0,s]; c0=offs[0,0,1,s]
-        q=c0//128; sh=c0-q*128
+        q=c0//128
+        return r0,q,c0-q*128
+    lane=lax.broadcasted_iota(jnp.int32,(R,128),1)
+    def begin(n,s):
+        r0,q,sh=place(s)
         keep=lane<128-sh
-        o=[]
-        for ch in range(2):
-            x=[pltpu.roll(ext[ch,q+j,pl.ds(r0,W),:],128-sh,1) for j in range(3)]
-            o.append(jnp.concatenate([jnp.where(keep,x[0],x[1]),jnp.where(keep,x[1],x[2])],axis=1))
-        orr,oi=o
-        pr=probe[0]; pi=probe[1]
-        return (s,on,r0,q,sh,orr,oi),(pr*orr-pi*oi,pr*oi+pi*orr)
-    def middle(st,a):
-        ar,ai=a
-        s,on=st[:2]
-        res=(ar*ar+ai*ai-mv[s])
-        if on is not None: res=res*on
-        return res*ar,res*ai
-    def close_slot(st,a):
-        s,on,r0,q,sh,orr,oi=st
-        br,bi=a
-        pr=probe[0]; pi=probe[1]
-        pg[0]+=orr*br+oi*bi
-        pg[1]+=orr*bi-oi*br
-        il=orr*orr+oi*oi
-        pg[2]+=il if on is None else il*on
-        gr=pr*br+pi*bi; gi=pr*bi-pi*br
+        parts=[]
+        for c in range(0,W,R):
+            o=[]
+            for ch in range(2):
+                x=[pltpu.roll(ext[ch,q+j,pl.ds(r0+c,R),:],128-sh,1) for j in range(3)]
+                o.append(jnp.concatenate([jnp.where(keep,x[0],x[1]),jnp.where(keep,x[1],x[2])],axis=1))
+                win[n,ch,c:c+R,:]=o[ch]
+            a,b=o; pr=probe[0,c:c+R,:]; pi=probe[1,c:c+R,:]
+            parts.append(cols(pr*a-pi*b,pr*b+pi*a))
+        return parts
+    def middle(uv,s,on):
+        parts={}
+        for c,yr,yi in rows(uv):
+            res=yr*yr+yi*yi-mv[s,c:c+R,:]
+            if on is not None: res=res*on
+            parts[c]=cols(res*yr,res*yi)
+        return [parts[c] for c in sorted(parts)]
+    def finish(n,uv,s,on):
+        r0,q,sh=place(s)
         low=lane<sh
-        for ch,g in enumerate((gr,gi)):
-            a=pltpu.roll(g[:,:128],sh,1); b=pltpu.roll(g[:,128:],sh,1)
-            z=jnp.zeros_like(a)
-            grad[ch,q,pl.ds(r0,W),:]+=jnp.where(low,z,a)
-            grad[ch,q+1,pl.ds(r0,W),:]+=jnp.where(low,a,b)
-            grad[ch,q+2,pl.ds(r0,W),:]+=jnp.where(low,b,z)
+        for c,br,bi in rows(uv):
+            a=win[n,0,c:c+R,:]; b=win[n,1,c:c+R,:]
+            pr=probe[0,c:c+R,:]; pi=probe[1,c:c+R,:]
+            pg[0,c:c+R,:]+=a*br+b*bi
+            pg[1,c:c+R,:]+=a*bi-b*br
+            il=a*a+b*b
+            pg[2,c:c+R,:]+=il if on is None else il*on
+            for ch,g in enumerate((pr*br+pi*bi,pr*bi-pi*br)):
+                x=pltpu.roll(g[:,:128],sh,1); y=pltpu.roll(g[:,128:],sh,1)
+                z=jnp.zeros_like(x)
+                at=pl.ds(r0+c,R)
+                grad[ch,q,at,:]+=jnp.where(low,z,x)
+                grad[ch,q+1,at,:]+=jnp.where(low,x,y)
+                grad[ch,q+2,at,:]+=jnp.where(low,y,z)
     def pair(p,_):
-        on=(2*p+1<live[0,0]).astype(jnp.float32)
-        sts,vs=zip(*[open_slot(2*p,None),open_slot(2*p+1,on)])
-        vs=[right_mul(*v,th,tl,0) for v in vs]
-        vs=[left_mul(*v,th,tl,0) for v in vs]
-        vs=[middle(st,v) for st,v in zip(sts,vs)]
-        vs=[right_mul(*v,th,tl,1) for v in vs]
-        vs=[left_mul(*v,th,tl,1) for v in vs]
-        for st,v in zip(sts,vs): close_slot(st,v)
+        two=[(0,2*p,None),(1,2*p+1,(2*p+1<live[0,0]).astype(jnp.float32))]
+        v=[right(begin(n,s),0) for n,s,_ in two]
+        v=[left(x,0) for x in v]
+        v=[right(middle(x,s,on),1) for x,(n,s,on) in zip(v,two)]
+        v=[left(x,1) for x in v]
+        for x,(n,s,on) in zip(v,two): finish(n,x,s,on)
         return 0
     lax.fori_loop(0,(live[0,0]+1)//2,pair,0)
 
-def compute(offs,live,ext,probe,meas,hi,lo):
+def compute(offs,live,ext,probe,meas,hi,lo,g0,pg0):
     f=jnp.float32
     sd=jax.ShapeDtypeStruct
     V=pl.BlockSpec(memory_space=pltpu.VMEM); M=pl.BlockSpec(memory_space=pltpu.SMEM)
     return pl.pallas_call(kernel,
         out_shape=[sd((2,6,T+W,128),f),sd((3,W,W),f)],
-        in_specs=[M,M,V,V,V,V,V],out_specs=[V,V],
+        in_specs=[M,M,V,V,V,V,V,V,V],out_specs=[V,V],input_output_aliases={7:0,8:1},scratch_shapes=[pltpu.VMEM((2,2,W,W),f)],
         compiler_params=pltpu.CompilerParams(vmem_limit_bytes=VM2*2**20),
-    )(jnp.swapaxes(offs,2,3),live,ext,probe,meas,hi,lo)
+    )(jnp.swapaxes(offs,2,3),live,ext,probe,meas,hi,lo,g0,pg0)
 
 
 VM1, VM3, NC = 4, 16, 64
@@ -141,7 +181,7 @@
     return barrier
 
 
-def halo_kernel(tile, probe, meas, th, tl, ext, probev, measv, thv, tlv, hop1, hop2, loc, snd, rcv):
+def halo_kernel(tile, probe, meas, th, tl, ext, probev, measv, thv, tlv, g0, pg0, hop1, hop2, zg, zp, loc, snd, rcv):
     row, col, up, down, left, right = places()
     loads = []
 
@@ -177,6 +217,11 @@
         load(tile.at[:, :, lanes(cb)], ext.at[:, cb, pl.ds(0, T), :])
     for src, dst in ((probe, probev), (meas, measv), (th, thv), (tl, tlv)):
         load(src, dst)
+    zg[...] = jnp.zeros_like(zg)
+    zp[...] = jnp.zeros_like(zp)
+    for cb in range(6):
+        load(zg, g0.at[:, cb])
+    load(zp, pg0)
     second, third, x = [], [], []
     for k in range(2):
         first[k].wait_recv()
@@ -200,9 +245,9 @@
     sd = jax.ShapeDtypeStruct
     H = W // 2
     same = [sd(a.shape, a.dtype) for a in (probe, meas, th, tl)]
-    return pl.pallas_call(lambda *a: halo_kernel(*a), out_shape=[sd((2, 6, T + W, 128), f), *same],
-        in_specs=[pl.BlockSpec(memory_space=pltpu.HBM)] * 5, out_specs=[A] * 5,
-        scratch_shapes=[pltpu.VMEM((2, 2, H, 128), f), pltpu.VMEM((2, 2, H, 128), f), pltpu.SemaphoreType.DMA((8,)), pltpu.SemaphoreType.DMA((13,)), pltpu.SemaphoreType.DMA((13,))],
+    return pl.pallas_call(lambda *a: halo_kernel(*a), out_shape=[sd((2, 6, T + W, 128), f), *same, sd((2, 6, T + W, 128), f), sd((3, W, W), f)],
+        in_specs=[pl.BlockSpec(memory_space=pltpu.HBM)] * 5, out_specs=[A] * 7,
+        scratch_shapes=[pltpu.VMEM((2, 2, H, 128), f), pltpu.VMEM((2, 2, H, 128), f), pltpu.VMEM((2, T + W, 128), f), pltpu.VMEM((3, W, W), f), pltpu.SemaphoreType.DMA((16,)), pltpu.SemaphoreType.DMA((13,)), pltpu.SemaphoreType.DMA((13,))],
         compiler_params=pltpu.CompilerParams(collective_id=0, has_side_effects=True, vmem_limit_bytes=VM1*2**20))(*[pltpu.with_memory_space_constraint(a, pltpu.HBM) for a in (tile, probe, meas, th, tl)])
 
 
@@ -464,8 +509,8 @@
 
 def local(specimen, probe_field, measured, offsets, live_counts):
     hi, lo = tables()
-    ext, probe, meas, hi, lo = halos(specimen, probe_field, measured[0, 0], jnp.asarray(hi), jnp.asarray(lo))
-    g, pg = compute(offsets, live_counts, ext, probe, meas, hi, lo)
+    ext, probe, meas, hi, lo, g0, pg0 = halos(specimen, probe_field, measured[0, 0], jnp.asarray(hi), jnp.asarray(lo))
+    g, pg = compute(offsets, live_counts, ext, probe, meas, hi, lo, g0, pg0)
     rrv, brv, step = spills(g, pg, lax.axis_size("row"), lax.axis_size("col"))
     return tuple(join(g, rrv, brv, step))
 

time: 72.4 us -> 72.3 us (level)
    pallas_call x1, Pallas kernels: 11.2 us -> 5.52 us  [compute(): pl.pallas_call(kernel, out_shape=[sd((2, 6, T + W, 128), f), sd((3, W, W)...]
    pallas_call x1, Pallas kernels: 33.2 us -> 38.6 us  [spills(): pl.pallas_call(lambda *a: spill_kernel(*a), out_shape=[sd((2, 2, T, 128),...]
where the time goes in v7:
time: 72.3 us; the launch traced here: 72.2 us
  Pallas kernels  70.9 us (98%)
  between operations  1.32 us (2%)
    pallas_call x1, Pallas kernels, spills(): pl.pallas_call(lambda *a: spill_kernel(*a), out_shape=[sd((2, 2, T, 128),...  38.6 us
    pallas_call x1, Pallas kernels, halos(): pl.pallas_call(lambda *a: halo_kernel(*a), out_shape=[sd((2, 6, T + W, 12...  25.2 us
    pallas_call x1, Pallas kernels, compute(): pl.pallas_call(kernel, out_shape=[sd((2, 6, T + W, 128), f), sd((3, W, W)...  5.52 us
    pallas_call x1, Pallas kernels, join(): pl.pallas_call(join_kernel, out_shape=[sd((2, T, T), f), sd((2, W, W), f)...  1.53 us

profile of v7, /device:TPU:1, one launch (start us, length us, event | category | flops | bytes accessed | tf_op | source)
XLA Modules:
  0.0 72.2 jit_solution(9870658982186836961)
XLA Ops:
  1.3 0.0 copy-start
  1.3 25.2 %shard_map.86 = (f32[2,6,768,128]{3,2,1,0:T(8,128)S(1)}, f32[2,256,256]{2,1,0:T(8,128)S(1)}, f32[8,256,256]{2,1,0:T(8,128)S(1)}, bf16[2,2,256,256]{3,2,1,0:T(8,1...) custom-call(f32[2,512,512]{2,1,0:T(8,128)} %a_0_.1, ...), custom_call_target="tpu_custom_call" | custom-call | tf_op jit(solution)/shard_map/pallas_call | solution.py:248
  26.5 0.0 copy-done
  26.5 5.5 %shard_map.87 = (f32[2,6,768,128]{3,2,1,0:T(8,128)S(1)}, f32[3,256,256]{2,1,0:T(8,128)S(1)}) custom-call(s32[1,1,2,8]{3,2,1,0:T(2,128)S(1)} %bitcast.2, s32[1,1]{1,0:T(1,128)S(6)} %copy.13.live, f32[2,6,768,128]{3,2,1,0:T(8,128)S(1)} %get-tuple-element.14.ext, ...), custom_call_target="tpu_custom_call", output_to_operand_aliasing={{0}: (7, {}), {1}: (8, {})} | custom-call | tf_op jit(solution)/shard_map/pallas_call | solution.py:154
  32.0 38.6 %shard_map.88 = (f32[2,2,512,128]{3,2,1,0:T(8,128)S(1)}, f32[2,4,256,128]{3,2,1,0:T(8,128)S(1)}, f32[2,256,256]{2,1,0:T(8,128)S(1)}) custom-call(f32[2,6,768,128]{3,2,1,0:T(8,128)S(1)} %get-tuple-element.21.a_0_.g, f32[3,256,256]{2,1,0:T(8,128)S(1)} %get-tuple-element.22.a_1_), custom_call_target="tpu_custom_call" | custom-call | tf_op jit(solution)/shard_map/pallas_call | solution.py:472
  70.7 1.5 %shard_map.89 = (f32[2,512,512]{2,1,0:T(8,128)}, f32[2,256,256]{2,1,0:T(8,128)}) custom-call(f32[2,6,768,128]{3,2,1,0:T(8,128)S(1)} %get-tuple-element.21.a_0_.g, f32[2,2,512,128]{3,2,1,0:T(8,128)S(1)} %get-tuple-element.23.rrv, f32[2,4,256,128]{3,2,1,0:T(8,128)S(1)} %get-tuple-element.24.brv, f32[2,256,256]{2,1,0:T(8,128)S(1)} %get-tuple-element.25.stepv), custom_call_target="tpu_custom_call" | custom-call | tf_op jit(solution)/shard_map/pallas_call | solution.py:504
Async XLA Ops:
  1.3 25.2 %copy-start = (s32[1,1,8,2]{2,3,1,0:T(2,128)S(1)}, s32[1,1,8,2]{2,3,1,0:T(2,128)}, u32[]{:S(2)}) copy-start(s32[1,1,8,2]{2,3,1,0:T(2,128)} %param.10) | copy-start | bytes 196

commit v8 on v7

--- a/solution.py
+++ b/solution.py
@@ -272,8 +272,9 @@
 
     sib = at(x, z, 1 - core)
     zm = at(x, z + depth - 1, core)
-    around = at(x + jnp.where(z == 1, 1, 0), z + depth - 1, 0)
-    source = at(x + jnp.where(z == 0, wide - 1, 0), z + 1, 1)
+    turn = at(x + jnp.where(z == 2, 1, 0), z + depth - 1, 1)
+    around = at(x, z + depth - 1, 0)
+    source = at(x, z + 1, 1)
     ys = [((row + k) % rows, col) for k in range(1, 4)]
     barrier = greet((left, sib, *ys))
 
@@ -324,7 +325,7 @@
         if level == 0:
             return put(g.at[:, 5, zrows[k], :], zhop1.at[k], zsnd.at[k], zrcv.at[k], zm)
         if level == 1:
-            return put(zhop1.at[k], zhop2.at[k], zsnd.at[3 + k], zrcv.at[3 + k], zm)
+            return put(zhop1.at[k], zhop2.at[k], zsnd.at[3 + k], zrcv.at[3 + k], turn)
         return put(zhop2.at[k], rrv.at[:, 1, zrows[k], :], zsnd.at[6 + k], zrcv.at[6 + k], around)
 
     def zdirect(k):

time: 72.3 us -> 71.3 us (0.986)
  Pallas kernels: 70.9 us -> 70.1 us
    pallas_call x1, Pallas kernels: 38.6 us -> 37.9 us  [spills(): pl.pallas_call(lambda *a: spill_kernel(*a), out_shape=[sd((2, 2, T, 128),...]
where the time goes in v8:
time: 71.3 us; the launch traced here: 71.4 us
  Pallas kernels  70.1 us (98%)
  between operations  1.32 us (2%)
    pallas_call x1, Pallas kernels, spills(): pl.pallas_call(lambda *a: spill_kernel(*a), out_shape=[sd((2, 2, T, 128),...  37.9 us
    pallas_call x1, Pallas kernels, halos(): pl.pallas_call(lambda *a: halo_kernel(*a), out_shape=[sd((2, 6, T + W, 12...  25.2 us
    pallas_call x1, Pallas kernels, compute(): pl.pallas_call(kernel, out_shape=[sd((2, 6, T + W, 128), f), sd((3, W, W)...  5.53 us
    pallas_call x1, Pallas kernels, join(): pl.pallas_call(join_kernel, out_shape=[sd((2, T, T), f), sd((2, W, W), f)...  1.53 us

profile of v8, /device:TPU:1, one launch (start us, length us, event | category | flops | bytes accessed | tf_op | source)
XLA Modules:
  0.0 71.4 jit_solution(12126797993042198998)
XLA Ops:
  1.3 0.0 copy-start
  1.3 25.2 %shard_map.86 = (f32[2,6,768,128]{3,2,1,0:T(8,128)S(1)}, f32[2,256,256]{2,1,0:T(8,128)S(1)}, f32[8,256,256]{2,1,0:T(8,128)S(1)}, bf16[2,2,256,256]{3,2,1,0:T(8,1...) custom-call(f32[2,512,512]{2,1,0:T(8,128)} %a_0_.1, ...), custom_call_target="tpu_custom_call" | custom-call | tf_op jit(solution)/shard_map/pallas_call | solution.py:248
  26.5 0.0 copy-done
  26.5 5.5 %shard_map.87 = (f32[2,6,768,128]{3,2,1,0:T(8,128)S(1)}, f32[3,256,256]{2,1,0:T(8,128)S(1)}) custom-call(s32[1,1,2,8]{3,2,1,0:T(2,128)S(1)} %bitcast.2, s32[1,1]{1,0:T(1,128)S(6)} %copy.13.live, f32[2,6,768,128]{3,2,1,0:T(8,128)S(1)} %get-tuple-element.14.ext, ...), custom_call_target="tpu_custom_call", output_to_operand_aliasing={{0}: (7, {}), {1}: (8, {})} | custom-call | tf_op jit(solution)/shard_map/pallas_call | solution.py:154
  32.0 37.9 %shard_map.88 = (f32[2,2,512,128]{3,2,1,0:T(8,128)S(1)}, f32[2,4,256,128]{3,2,1,0:T(8,128)S(1)}, f32[2,256,256]{2,1,0:T(8,128)S(1)}) custom-call(f32[2,6,768,128]{3,2,1,0:T(8,128)S(1)} %get-tuple-element.21.a_0_.g, f32[3,256,256]{2,1,0:T(8,128)S(1)} %get-tuple-element.22.a_1_), custom_call_target="tpu_custom_call" | custom-call | tf_op jit(solution)/shard_map/pallas_call | solution.py:473
  69.9 1.5 %shard_map.89 = (f32[2,512,512]{2,1,0:T(8,128)}, f32[2,256,256]{2,1,0:T(8,128)}) custom-call(f32[2,6,768,128]{3,2,1,0:T(8,128)S(1)} %get-tuple-element.21.a_0_.g, f32[2,2,512,128]{3,2,1,0:T(8,128)S(1)} %get-tuple-element.23.rrv, f32[2,4,256,128]{3,2,1,0:T(8,128)S(1)} %get-tuple-element.24.brv, f32[2,256,256]{2,1,0:T(8,128)S(1)} %get-tuple-element.25.stepv), custom_call_target="tpu_custom_call" | custom-call | tf_op jit(solution)/shard_map/pallas_call | solution.py:505
Async XLA Ops:
  1.3 25.2 %copy-start = (s32[1,1,8,2]{2,3,1,0:T(2,128)S(1)}, s32[1,1,8,2]{2,3,1,0:T(2,128)}, u32[]{:S(2)}) copy-start(s32[1,1,8,2]{2,3,1,0:T(2,128)} %param.10) | copy-start | bytes 196
